TPU v7x, 32 devices: a whole 2x2x4 slice. The times are simulated.
32 devices in a mesh: rep: 2 (over x), shard: 16 (over z, y, core).
Axes of the slice: x: 2, y: 2, z: 4, core: 2. Of those that a mesh axis runs over, the one named last changes fastest.
Arguments:
- tokens: bfloat16 [16384, 1024], P(('shard', 'rep')), may hold values from -6 to 6
- segments: int32 [16384], P(('shard', 'rep')), may hold values from 0 to 17, as said below
- cotangent: bfloat16 [16384, 1024], P(('shard', 'rep')), may hold values from -6 to 6
- w_qkv: float32 [1024, 3072], P('shard'), may hold values from -0.1875 to 0.1875
- b_qkv: float32 [3072], P('shard'), may hold values from -1.2 to 1.2
- w_out: float32 [1024, 1024], P('shard'), may hold values from -1 to 1
- b_out: float32 [1024], P('shard'), may hold values from -1.2 to 1.2
- gain_one: float32 [1024], P('shard'), may hold values from 0.5 to 1.5
- shift_one: float32 [1024], P('shard'), may hold values from -1.2 to 1.2
- w_up: float32 [1024, 4096], P('shard'), may hold values from -0.1875 to 0.1875
- b_up: float32 [4096], P('shard'), may hold values from -1.2 to 1.2
- w_down: float32 [4096, 1024], P('shard'), may hold values from -0.09375 to 0.09375
- b_down: float32 [1024], P('shard'), may hold values from -1.2 to 1.2
- gain_two: float32 [1024], P('shard'), may hold values from 0.5 to 1.5
- shift_two: float32 [1024], P('shard'), may hold values from -1.2 to 1.2
Outputs:
- result: bfloat16 [16384, 1024], P(('shard', 'rep'))
- input_grad: float32 [16384, 1024], P(('shard', 'rep'))
- grad_w_qkv: float32 [1024, 3072], P('shard')
- grad_b_qkv: float32 [3072], P('shard')
- grad_w_out: float32 [1024, 1024], P('shard')
- grad_b_out: float32 [1024], P('shard')
- grad_gain_one: float32 [1024], P('shard')
- grad_shift_one: float32 [1024], P('shard')
- grad_w_up: float32 [1024, 4096], P('shard')
- grad_b_up: float32 [4096], P('shard')
- grad_w_down: float32 [4096, 1024], P('shard')
- grad_b_down: float32 [1024], P('shard')
- grad_gain_two: float32 [1024], P('shard')
- grad_shift_two: float32 [1024], P('shard')
Inputs may be any that keep to these rules, and one draw needn't show every extreme that they name: `segments`: within each sequence of 1024 slots the segment numbers start at 0, never fall and rise by one from one document to the next; every document has 60 to 800 slots except the last of its sequence, which may be shorter; some document has exactly 800 slots.
All inputs are finite; a program needn't handle non-finite values.
Results may differ from a plain program's by a relative error of at most 0.015.
The roundings to bfloat16 on the way count: a program that leaves them out, or rounds other values in their place, can miss the bound.
Values may be sent and summed in bfloat16 or wider, within the bound.
A program may use at most 192 MiB of HBM per device.

v0:
```python
import math

import jax
import jax.numpy as jnp
from jax import lax
from jax.sharding import PartitionSpec as P

D = 1024
HEADS = 16
HEAD_DIM = 64


group_heads = 4


def from_partner(value, axis, stride):
    mask = 2**stride
    pairs = [(source, source ^ mask) for source in range(lax.axis_size(axis))]
    return lax.ppermute(value, axis, pairs)


def turn(vectors):
    halfway = vectors.shape[-1] // 2
    return jnp.concatenate([-vectors[..., halfway:], vectors[..., :halfway]], axis=-1)


def turn_back(vectors):
    halfway = vectors.shape[-1] // 2
    return jnp.concatenate([vectors[..., halfway:], -vectors[..., :halfway]], axis=-1)


def rope_tables(first_pos, tok_count):
    position = (first_pos + jnp.arange(tok_count, dtype=jnp.int32)).astype(jnp.float32)
    frequency = jnp.exp(
        jnp.arange(HEAD_DIM // 2, dtype=jnp.float32) * (-2.0 * math.log(10000.0) / HEAD_DIM)
    )
    angles = position[:, None] * frequency[None, :]
    angles = jnp.concatenate([angles, angles], axis=1)
    return (jnp.cos(angles), jnp.sin(angles))


def rotate_rows(vectors, cosine, sine_table):
    shaped = vectors.reshape(vectors.shape[0], HEADS, HEAD_DIM)
    rotated = shaped * cosine[:, None, :] + turn(shaped) * sine_table[:, None, :]
    return rotated.reshape(vectors.shape[0], D)


def rotate_back(grad_rows, cosine, sine_table):
    shaped = grad_rows.reshape(grad_rows.shape[0], HEADS, HEAD_DIM)
    rotated = shaped * cosine[:, None, :] + turn_back(shaped * sine_table[:, None, :])
    return rotated.reshape(grad_rows.shape[0], D)


def normalize(residual, gain_vec, shift_vec):
    mean_val = jnp.mean(residual, axis=-1, keepdims=True)
    centred = residual - mean_val
    variance = jnp.mean(centred * centred, axis=-1, keepdims=True)
    inv_std = lax.rsqrt(variance + 1e-05)
    normed = centred * inv_std
    return (normed * gain_vec + shift_vec, normed, inv_std)


def normalize_back(upstream, normed, inv_std, gain_vec):
    scaled = upstream * gain_vec
    d_input = inv_std * (
        scaled
        - jnp.mean(scaled, axis=-1, keepdims=True)
        - normed * jnp.mean(scaled * normed, axis=-1, keepdims=True)
    )
    return (d_input, jnp.sum(upstream * normed, axis=0), jnp.sum(upstream, axis=0))


def gelu_exact(values):
    return jax.nn.gelu(values, approximate=False)


def local(
    tokens,
    segments,
    cotangent,
    w_qkv,
    b_qkv,
    w_out,
    b_out,
    gain_one,
    shift_one,
    w_up,
    b_up,
    w_down,
    b_down,
    gain_two,
    shift_two,
):
    bf16 = jnp.bfloat16
    f32 = jnp.float32
    tok_rows = tokens.shape[0]
    width_cols = group_heads * HEAD_DIM
    group_count = HEADS // group_heads
    score_scale = HEAD_DIM ** (-0.5)
    qkv_low = w_qkv.astype(bf16)
    qkvb_low = b_qkv.astype(bf16)
    out_low = w_out.astype(bf16)
    outb_low = b_out.astype(bf16)
    gaina_low = gain_one.astype(bf16)
    shifta_low = shift_one.astype(bf16)
    up_low = w_up.astype(bf16)
    upb_low = b_up.astype(bf16)
    down_low = w_down.astype(bf16)
    downb_low = b_down.astype(bf16)
    gainb_low = gain_two.astype(bf16)
    shiftb_low = shift_two.astype(bf16)
    qkv_w, qkv_b, out_w, out_b, gain_a, shift_a = (
        lax.all_gather(qkv_low, "shard", axis=0, tiled=True),
        lax.all_gather(qkvb_low, "shard", axis=0, tiled=True),
        lax.all_gather(out_low, "shard", axis=0, tiled=True),
        lax.all_gather(outb_low, "shard", axis=0, tiled=True),
        lax.all_gather(gaina_low, "shard", axis=0, tiled=True),
        lax.all_gather(shifta_low, "shard", axis=0, tiled=True),
    )
    seq_half = lax.axis_index("rep")
    cosine, sine_table = rope_tables(seq_half * tok_rows, tok_rows)
    inputs = tokens.astype(f32)
    joined = jnp.dot(tokens, qkv_w, preferred_element_type=f32) + qkv_b.astype(f32)
    queries = rotate_rows(joined[:, :D], cosine, sine_table).astype(bf16)
    keys_own = rotate_rows(joined[:, D : 2 * D], cosine, sine_table).astype(bf16)
    values_own = joined[:, 2 * D :].astype(bf16)
    doc_own = segments.astype(bf16)
    keys_peer, values_peer, doc_peer = from_partner((keys_own, values_own, doc_own), "rep", 0)
    keys_all = jnp.concatenate([keys_own, keys_peer], axis=0)
    values_all = jnp.concatenate([values_own, values_peer], axis=0)
    doc_all = jnp.concatenate([doc_own, doc_peer], axis=0)
    same_doc = doc_own[:, None] == doc_all[None, :]

    def head_block(buffer_in, column):
        return lax.dynamic_slice_in_dim(buffer_in, column, width_cols, 1).reshape(
            buffer_in.shape[0], group_heads, HEAD_DIM
        )

    def masked_scores(q_part, k_part):
        raw_scores = (
            jnp.einsum("thd,khd->htk", q_part, k_part, preferred_element_type=f32) * score_scale
        )
        return jnp.where(same_doc[None], raw_scores, -1e30)

    def attend(group_index, state_pair):
        context, log_total = state_pair
        column = group_index * width_cols
        masked = masked_scores(head_block(queries, column), head_block(keys_all, column))
        row_max = jnp.max(masked, axis=-1, keepdims=True)
        exponent = jnp.exp(masked - row_max)
        row_sum = jnp.sum(exponent, axis=-1, keepdims=True)
        prob_low = (exponent / row_sum).astype(bf16)
        mixed_part = jnp.einsum(
            "htk,khd->thd", prob_low, head_block(values_all, column), preferred_element_type=f32
        )
        context = lax.dynamic_update_slice_in_dim(
            context, mixed_part.reshape(tok_rows, width_cols), column, 1
        )
        log_total = lax.dynamic_update_slice_in_dim(
            log_total, (row_max + jnp.log(row_sum))[:, :, 0], group_index * group_heads, 0
        )
        return (context, log_total)

    context, log_total = lax.fori_loop(
        0, group_count, attend, (jnp.zeros((tok_rows, D), f32), jnp.zeros((HEADS, tok_rows), f32))
    )
    context_low = context.astype(bf16)
    attn_out = jnp.dot(context_low, out_w, preferred_element_type=f32) + out_b.astype(f32)
    gain_a32 = gain_a.astype(f32)
    first_norm, normed_a, inv_a = normalize(inputs + attn_out, gain_a32, shift_a.astype(f32))
    first_low = first_norm.astype(bf16)
    up_w, up_b, down_w, down_b, gain_b, shift_b = (
        lax.all_gather(up_low, "shard", axis=0, tiled=True),
        lax.all_gather(upb_low, "shard", axis=0, tiled=True),
        lax.all_gather(down_low, "shard", axis=0, tiled=True),
        lax.all_gather(downb_low, "shard", axis=0, tiled=True),
        lax.all_gather(gainb_low, "shard", axis=0, tiled=True),
        lax.all_gather(shiftb_low, "shard", axis=0, tiled=True),
    )
    hidden = jnp.dot(first_low, up_w, preferred_element_type=f32) + up_b.astype(f32)
    active_low = gelu_exact(hidden).astype(bf16)
    ffn_out = jnp.dot(active_low, down_w, preferred_element_type=f32) + down_b.astype(f32)
    gain_b32 = gain_b.astype(f32)
    final_out, normed_b, inv_b = normalize(first_norm + ffn_out, gain_b32, shift_b.astype(f32))
    qkv_w, qkv_b, out_w, out_b, gain_a, shift_a = (
        lax.all_gather(qkv_low, "shard", axis=0, tiled=True),
        lax.all_gather(qkvb_low, "shard", axis=0, tiled=True),
        lax.all_gather(out_low, "shard", axis=0, tiled=True),
        lax.all_gather(outb_low, "shard", axis=0, tiled=True),
        lax.all_gather(gaina_low, "shard", axis=0, tiled=True),
        lax.all_gather(shifta_low, "shard", axis=0, tiled=True),
    )
    up_w, up_b, down_w, down_b, gain_b, shift_b = (
        lax.all_gather(up_low, "shard", axis=0, tiled=True),
        lax.all_gather(upb_low, "shard", axis=0, tiled=True),
        lax.all_gather(down_low, "shard", axis=0, tiled=True),
        lax.all_gather(downb_low, "shard", axis=0, tiled=True),
        lax.all_gather(gainb_low, "shard", axis=0, tiled=True),
        lax.all_gather(shiftb_low, "shard", axis=0, tiled=True),
    )
    gain_a32 = gain_a.astype(f32)
    gain_b32 = gain_b.astype(f32)
    upstream = cotangent.astype(f32)
    d_second, gain_b_grad, shift_b_grad = normalize_back(upstream, normed_b, inv_b, gain_b32)
    d_ffn_low = d_second.astype(bf16)
    down_b_grad = jnp.sum(d_ffn_low.astype(f32), axis=0)
    down_w_grad = jnp.einsum("tf,td->fd", active_low, d_ffn_low, preferred_element_type=f32)
    d_active = jnp.einsum("td,fd->tf", d_ffn_low, down_w, preferred_element_type=f32)
    gelu_pull = jax.vjp(gelu_exact, hidden)[1]
    d_hidden_low = gelu_pull(d_active)[0].astype(bf16)
    up_b_grad = jnp.sum(d_hidden_low.astype(f32), axis=0)
    up_w_grad = jnp.einsum("td,tf->df", first_low, d_hidden_low, preferred_element_type=f32)
    d_first = d_second + jnp.einsum("tf,df->td", d_hidden_low, up_w, preferred_element_type=f32)
    d_resid, gain_a_grad, shift_a_grad = normalize_back(d_first, normed_a, inv_a, gain_a32)
    d_attn_low = d_resid.astype(bf16)
    out_b_grad = jnp.sum(d_attn_low.astype(f32), axis=0)
    out_w_grad = jnp.einsum("tc,td->cd", context_low, d_attn_low, preferred_element_type=f32)
    d_context_low = jnp.einsum("td,cd->tc", d_attn_low, out_w, preferred_element_type=f32).astype(
        bf16
    )

    def attend_back(group_index, state_triple):
        d_queries, d_keys, d_values = state_triple
        column = group_index * width_cols
        q_part = head_block(queries, column)
        k_part = head_block(keys_all, column)
        v_part = head_block(values_all, column)
        g_part = head_block(d_context_low, column)
        masked = masked_scores(q_part, k_part)
        log_part = lax.dynamic_slice_in_dim(log_total, group_index * group_heads, group_heads, 0)
        attn_prob = jnp.exp(masked - log_part[:, :, None])
        prob_low = attn_prob.astype(bf16)
        value_grad = jnp.einsum("htk,thd->khd", prob_low, g_part, preferred_element_type=f32)
        prob_grad = jnp.einsum("thd,khd->htk", g_part, v_part, preferred_element_type=f32)
        inner_sum = jnp.sum(attn_prob * prob_grad, axis=-1, keepdims=True)
        score_low = (attn_prob * (prob_grad - inner_sum)).astype(bf16)
        query_grad = (
            jnp.einsum("htk,khd->thd", score_low, k_part, preferred_element_type=f32) * score_scale
        )
        key_grad = (
            jnp.einsum("htk,thd->khd", score_low, q_part, preferred_element_type=f32) * score_scale
        )
        d_queries = lax.dynamic_update_slice_in_dim(
            d_queries, query_grad.reshape(tok_rows, width_cols), column, 1
        )
        d_keys = lax.dynamic_update_slice_in_dim(
            d_keys, key_grad.reshape(2 * tok_rows, width_cols), column, 1
        )
        d_values = lax.dynamic_update_slice_in_dim(
            d_values, value_grad.reshape(2 * tok_rows, width_cols), column, 1
        )
        return (d_queries, d_keys, d_values)

    start_state = (
        jnp.zeros((tok_rows, D), f32),
        jnp.zeros((2 * tok_rows, D), f32),
        jnp.zeros((2 * tok_rows, D), f32),
    )
    d_queries, d_keys, d_values = lax.fori_loop(0, group_count, attend_back, start_state)
    peer_dk, peer_dv = (
        from_partner(d_keys[tok_rows:].astype(jnp.bfloat16), "rep", 0).astype(jnp.float32),
        from_partner(d_values[tok_rows:].astype(jnp.bfloat16), "rep", 0).astype(jnp.float32),
    )
    d_keys_own = d_keys[:tok_rows] + peer_dk
    d_values_own = d_values[:tok_rows] + peer_dv
    d_joined_low = jnp.concatenate(
        [
            rotate_back(d_queries, cosine, sine_table),
            rotate_back(d_keys_own, cosine, sine_table),
            d_values_own,
        ],
        axis=1,
    ).astype(bf16)
    qkv_b_grad = jnp.sum(d_joined_low.astype(f32), axis=0)
    qkv_w_grad = jnp.einsum("td,te->de", tokens, d_joined_low, preferred_element_type=f32)
    input_grad = d_resid + jnp.einsum("te,de->td", d_joined_low, qkv_w, preferred_element_type=f32)
    attn_sums = (
        lax.psum_scatter(qkv_w_grad, "shard", scatter_dimension=0, tiled=True),
        lax.psum_scatter(qkv_b_grad, "shard", scatter_dimension=0, tiled=True),
        lax.psum_scatter(out_w_grad, "shard", scatter_dimension=0, tiled=True),
        lax.psum_scatter(out_b_grad, "shard", scatter_dimension=0, tiled=True),
        lax.psum_scatter(gain_a_grad, "shard", scatter_dimension=0, tiled=True),
        lax.psum_scatter(shift_a_grad, "shard", scatter_dimension=0, tiled=True),
    )
    ffn_sums = (
        lax.psum_scatter(up_w_grad, "shard", scatter_dimension=0, tiled=True),
        lax.psum_scatter(up_b_grad, "shard", scatter_dimension=0, tiled=True),
        lax.psum_scatter(down_w_grad, "shard", scatter_dimension=0, tiled=True),
        lax.psum_scatter(down_b_grad, "shard", scatter_dimension=0, tiled=True),
        lax.psum_scatter(gain_b_grad, "shard", scatter_dimension=0, tiled=True),
        lax.psum_scatter(shift_b_grad, "shard", scatter_dimension=0, tiled=True),
    )
    totals = (
        lax.psum(attn_sums[0].astype(jnp.bfloat16), "rep").astype(jnp.float32),
        lax.psum(attn_sums[1].astype(jnp.bfloat16), "rep").astype(jnp.float32),
        lax.psum(attn_sums[2].astype(jnp.bfloat16), "rep").astype(jnp.float32),
        lax.psum(attn_sums[3].astype(jnp.bfloat16), "rep").astype(jnp.float32),
        lax.psum(attn_sums[4].astype(jnp.bfloat16), "rep").astype(jnp.float32),
        lax.psum(attn_sums[5].astype(jnp.bfloat16), "rep").astype(jnp.float32),
        lax.psum(ffn_sums[0].astype(jnp.bfloat16), "rep").astype(jnp.float32),
        lax.psum(ffn_sums[1].astype(jnp.bfloat16), "rep").astype(jnp.float32),
        lax.psum(ffn_sums[2].astype(jnp.bfloat16), "rep").astype(jnp.float32),
        lax.psum(ffn_sums[3].astype(jnp.bfloat16), "rep").astype(jnp.float32),
        lax.psum(ffn_sums[4].astype(jnp.bfloat16), "rep").astype(jnp.float32),
        lax.psum(ffn_sums[5].astype(jnp.bfloat16), "rep").astype(jnp.float32),
    )
    return (
        final_out.astype(bf16),
        input_grad,
        totals[0],
        totals[1],
        totals[2],
        totals[3],
        totals[4],
        totals[5],
        totals[6],
        totals[7],
        totals[8],
        totals[9],
        totals[10],
        totals[11],
    )


def solution(mesh):
    return jax.shard_map(
        local,
        mesh=mesh,
        in_specs=(
            P(("shard", "rep"), None),
            P(("shard", "rep")),
            P(("shard", "rep"), None),
            P("shard", None),
            P("shard"),
            P("shard", None),
            P("shard"),
            P("shard"),
            P("shard"),
            P("shard", None),
            P("shard"),
            P("shard", None),
            P("shard"),
            P("shard"),
            P("shard"),
        ),
        out_specs=(
            P(("shard", "rep"), None),
            P(("shard", "rep"), None),
            P("shard", None),
            P("shard"),
            P("shard", None),
            P("shard"),
            P("shard"),
            P("shard"),
            P("shard", None),
            P("shard"),
            P("shard", None),
            P("shard"),
            P("shard"),
            P("shard"),
        ),
        check_vma=False,
    )
```

profile of v0, /device:TPU:0, one launch (start us, length us, event | category | flops | bytes accessed | tf_op | source)
XLA Modules:
  0.0 1098.9 jit_solution(17036748721458300454)
XLA Ops:
  16.8 64.4 %all-reduce.16 = (bf16[3072]{0:T(1024)(128)(2,1)S(1)}, bf16[1024]{0:T(1024)(128)(2,1)S(1)}, bf16[1024]{0:T(1024)(128)(2,1)S(1)}, bf16[1024]{0:T(1024)(128)(2,1)S...) all-reduce(bf16[3072]{0:T(1024)(128)(2,1)S(1)} %dynamic-update-slic, ...), channel_id=1, replica_groups=mesh['rep'=2,'shard'=16] {'shard'}, use_global_device_ids=true, to_apply=%add | all-reduce | flops 9216 | bytes 36864
  124.6 17.9 %all-gather = bf16[16,1,256]{2,1,0:T(2,128)(2,1)S(1)} all-gather(bf16[1,1,256]{2,1,0:T(2,128)(2,1)S(1)} %reshape.278), channel_id=1, replica_groups=mesh['rep'=2,'shard'=16] {'shard'}, dimensions={0}, use_global_device_ids=true | all-gather | bytes 8704 | tf_op jit(solution)/shard_map/all_gather | solution.py:174
  144.3 15.3 %collective-permute-done.1 = bf16[512]{0:T(512)(128)(2,1)S(1)} collective-permute-done((bf16[512]{0:T(512)(128)(2,1)S(1)}, bf16[512]{0:T(512)(128)(2,1)S(1)}, u32[]{:S(2)}, u32[]{:S(2)}) %collective-permute-start.1) | collective-permute-done | bytes 1056 | tf_op jit(solution)/shard_map/ppermute | solution.py:19
  173.6 61.9 %while.34 = (s32[]{:T(128)}, bf16[512,1024]{0,1:T(8,128)(2,1)}, f32[16,512]{1,0:T(8,128)S(1)}, bf16[1024,1024]{0,1:T(8,128)(2,1)}, bf16[512,1024]{0,1:T(8,128)(2...) while((s32[]{:T(128)}, bf16[512,1024]{0,1:T(8,128)(2,1)}, ...), condition=%wide.region_3.4_spmd.clone, body=%wide.region_0.3_spmd.clone.sunk | while | flops 562558976 | bytes 65604876 | solution.py:164
  240.7 28.1 %multiply_convert_fusion.1 = (bf16[512,4096]{1,0:T(8,128)(2,1)}, f32[512,4096]{1,0:T(8,128)}, f32[512,4096]{1,0:T(8,128)}) fusion(f32[4096]{0:T(1024)S(1)} %bitcast.143, bf16[1024,4096]{1,0:T(8,128)(2,1)} %all-gather.10.cloned.1.call-done, f32[512,1024]{1,0:T(8,128)} %copy-done.3, f32[1024]{0:T(1024)S(1)} %convert_element_type.238, ...), kind=kOutput, calls=%fused_computation.39 | convolution fusion | flops 4436000768 | bytes 31485952 | tf_op jit(solution)/shard_map/dot_general | solution.py:180
  270.6 10.0 fusion.55
  285.0 16.4 %convert_reduce_fusion = (f32[4096]{0:T(1024)}, bf16[512,4096]{1,0:T(8,128)(2,1)}) fusion(f32[512,4096]{1,0:T(8,128)} %get-tuple-element.538, bf16[4096,1024]{1,0:T(8,128)(2,1)} %all-gather.12.cloned.1.call-done, f32[512,1024]{1,0:T(8,128)S(1)} %get-tuple-element.534, f32[512,4096]{1,0:T(8,128)} %get-tuple-element.572, f32[4096]{0:T(1024)S(1)} %bitcast.144), kind=kOutput, calls=%fused_computation.37 | convolution fusion | flops 4331139072 | bytes 31490048 | tf_op jit(solution)/shard_map/td,fd->tf/dot_general | solution.py:208
  301.4 9.6 multiply_reduce_fusion.1
  329.3 100.2 %while.35 = (s32[]{:T(128)}, f32[512,1024]{0,1:T(8,128)}, f32[1024,1024]{0,1:T(8,128)}, f32[1024,1024]{0,1:T(8,128)}, bf16[1024,1024]{0,1:T(8,128)(2,1)S(1)}, /*...) while((s32[]{:T(128)}, f32[512,1024]{0,1:T(8,128)}, ...), condition=%wide.region_14.15_spmd.clone, body=%wide.region_12.0_spmd.clone.sunk | while | flops 1374550016 | bytes 121171320 | solution.py:259
  339.2 5.8 multiply_reduce_fusion.7
  364.1 5.8 multiply_reduce_fusion.7
  389.0 5.9 multiply_reduce_fusion.7
  413.9 5.8 multiply_reduce_fusion.7
  435.3 22.2 %collective-permute-done.3 = bf16[512,1024]{0,1:T(8,128)(2,1)S(1)} collective-permute-done((bf16[512,1024]{0,1:T(8,128)(2,1)S(1)}, bf16[512,1024]{0,1:T(8,128)(2,1)S(1)}, u32[]{:S(2)}, u32[]{:S(2)}) %collective-permute-start.3) | collective-permute-done | bytes 1048608 | tf_op jit(solution)/shard_map/ppermute | solution.py:19
  464.2 15.1 %collective-permute-done.4 = bf16[512,1024]{0,1:T(8,128)(2,1)S(1)} collective-permute-done((bf16[512,1024]{0,1:T(8,128)(2,1)S(1)}, bf16[512,1024]{0,1:T(8,128)(2,1)S(1)}, u32[]{:S(2)}, u32[]{:S(2)}) %collective-permute-start.4) | collective-permute-done | bytes 1048608 | tf_op jit(solution)/shard_map/ppermute | solution.py:19
  479.7 10.0 convolution_bitcast_fusion
  489.7 12.6 %copy.71 = f32[1024,3072]{1,0:T(8,128)} copy(f32[1024,3072]{0,1:T(8,128)} %convolution_bitcast_fusion) | data formatting | bytes 25165824
  503.9 12.6 %fusion.44 = f32[1024,4096]{1,0:T(8,128)} fusion(bf16[512,4096]{1,0:T(8,128)(2,1)} %get-tuple-element.577, f32[512,1024]{1,0:T(8,128)S(1)} %copy-done.5, f32[1024]{0:T(1024)S(1)} %copy-done.39, f32[1024]{0:T(1024)S(1)} %copy-done.29, f32[512]{0:T(512)S(1)} %copy-done.37, f32[512]{0:T(512)S(1)} %copy-done.27), kind=kOutput, calls=%fused_computation.142 | convolution fusion | flops 4297588736 | bytes 23080960 | tf_op jit(solution)/shard_map/td,tf->df/dot_general | solution.py:212
  518.4 11.4 %fusion.38 = f32[4096,1024]{1,0:T(8,128)} fusion(bf16[512,4096]{1,0:T(8,128)(2,1)} %get-tuple-element.537, f32[512,1024]{1,0:T(8,128)S(1)} %copy-done.16), kind=kOutput, calls=%fused_computation.138 | convolution fusion | flops 4295491584 | bytes 23068672 | tf_op jit(solution)/shard_map/tf,td->fd/dot_general | solution.py:207
  531.5 104.8 %reduce-scatter.13.cloned.1.call-done = f32[64,3072]{1,0:T(8,128)} async-done(((f32[1024,3072]{1,0:T(8,128)}), f32[64,3072]{1,0:T(8,128)}) %reduce-scatter.13.cloned.1.call-update) | async-done | bytes 786448
  638.6 180.1 %reduce-scatter.9.cloned.1.call-done = f32[64,4096]{1,0:T(8,128)} async-done(((f32[1024,4096]{1,0:T(8,128)}), f32[64,4096]{1,0:T(8,128)}) %reduce-scatter.9.cloned.1.call-update) | async-done | bytes 1048592 | tf_op jit(solution)/shard_map/reduce_scatter | solution.py:286
  820.8 180.1 %reduce-scatter.11.cloned.1.call-done = f32[256,1024]{1,0:T(8,128)} async-done(((f32[4096,1024]{1,0:T(8,128)}), f32[256,1024]{1,0:T(8,128)}) %reduce-scatter.11.cloned.1.call-update) | async-done | bytes 1048592 | tf_op jit(solution)/shard_map/reduce_scatter | solution.py:288
  1007.2 59.7 %all-reduce.15 = (bf16[3072]{0:T(1024)(128)(2,1)S(1)}, bf16[1024]{0:T(1024)(128)(2,1)S(1)}, bf16[1024]{0:T(1024)(128)(2,1)S(1)}, bf16[1024]{0:T(1024)(128)(2,1)S...) all-reduce(f32[3072]{0:T(1024)S(1)} %convert_reduce_fusion.1, ...), channel_id=3, replica_groups=mesh['rep'=2,'shard'=16] {'shard'}, use_global_device_ids=true, to_apply=%region_18.19.clone | all-reduce | flops 13312 | bytes 79872
  1076.7 8.2 convolution_add_fusion.1
  (379 shorter events, 277.8 us)
Async XLA Ops:
  7.3 77.0 %all-gather.6.cloned.1.call-start = ((), (), s32[]{:S(2)}) async-start(), calls=%async_computation.4 | async-start | bytes 6684672 | tf_op jit(solution)/shard_map/all_gather | solution.py:113
  9.3 226.2 %all-gather.8.cloned.1.call-start = ((), (), s32[]{:S(2)}) async-start(), calls=%async_computation.5 | async-start | bytes 2228224 | tf_op jit(solution)/shard_map/all_gather | solution.py:115
  11.0 229.7 %all-gather.10.cloned.1.call-start = ((), (), s32[]{:S(2)}) async-start(), calls=%async_computation.6 | async-start | bytes 8912896 | tf_op jit(solution)/shard_map/all_gather | solution.py:173
  13.2 257.4 %all-gather.12.cloned.1.call-start = ((), (), s32[]{:S(2)}) async-start(), calls=%async_computation.7 | async-start | bytes 8912896 | tf_op jit(solution)/shard_map/all_gather | solution.py:175
  116.4 44.6 %collective-permute-start.2 = (bf16[512,1024]{1,0:T(8,128)(2,1)}, bf16[512,1024]{1,0:T(8,128)(2,1)S(1)}, u32[]{:S(2)}, u32[]{:S(2)}) collective-permute-start(bf16[512,1024]{1,0:T(8,128)(2,1)} %get-tuple-element.547), channel_id=1, source_target_pairs={{0,16},{16,0},{1,17},{17,1},{2,18},{18,2},{3,19},{19,3},{4,20},{20... | collective-permute-start | bytes 3145736 | tf_op jit(solution)/shard_map/ppermute | solution.py:19
  120.6 46.0 %collective-permute-start = (bf16[512,1024]{1,0:T(8,128)(2,1)}, bf16[512,1024]{1,0:T(8,128)(2,1)}, u32[]{:S(2)}, u32[]{:S(2)}) collective-permute-start(bf16[512,1024]{1,0:T(8,128)(2,1)} %slice.89), channel_id=1, source_target_pairs={{0,16},{16,0},{1,17},{17,1},{2,18},{18,2},{3,19},{19,3},{4,20},{20... | collective-permute-start | bytes 3145736 | tf_op jit(solution)/shard_map/ppermute | solution.py:19
  121.1 38.5 %collective-permute-start.1 = (bf16[512]{0:T(512)(128)(2,1)S(1)}, bf16[512]{0:T(512)(128)(2,1)S(1)}, u32[]{:S(2)}, u32[]{:S(2)}) collective-permute-start(bf16[512]{0:T(512)(128)(2,1)S(1)} %convert_element_type.227), channel_id=1, source_target_pairs={{0,16},{16,0},{1,17},{17,1},{2,18},{18,2},{3,19},{19,3},{4,20},{20... | collective-permute-start | bytes 3080 | tf_op jit(solution)/shard_map/ppermute | solution.py:19
  123.5 406.4 %reduce-scatter.7.cloned.1.call-start = ((), (), s32[]{:S(2)}) async-start(), calls=%async_computation.8 | async-start | bytes 4456448 | tf_op jit(solution)/shard_map/reduce_scatter | solution.py:280
  142.5 168.5 %copy-start.28 = (f32[1024]{0:T(1024)}, f32[1024]{0:T(1024)S(1)}, u32[]{:S(2)}) copy-start(f32[1024]{0:T(1024)S(1)} %convert_element_type.236) | copy-start | bytes 12292
  142.5 128.1 %copy-start.38 = (f32[1024]{0:T(1024)}, f32[1024]{0:T(1024)S(1)}, u32[]{:S(2)}) copy-start(f32[1024]{0:T(1024)S(1)} %convert_element_type.238) | copy-start | bytes 12292
  318.2 318.1 %reduce-scatter.13.cloned.1.call-start = ((), (), s32[]{:S(2)}) async-start(), calls=%async_computation.11 | async-start | bytes 13369344
  431.4 26.1 %collective-permute-start.3 = (bf16[512,1024]{0,1:T(8,128)(2,1)S(1)}, bf16[512,1024]{0,1:T(8,128)(2,1)S(1)}, u32[]{:S(2)}, u32[]{:S(2)}) collective-permute-start(bf16[512,1024]{0,1:T(8,128)(2,1)S(1)} %slice.88), channel_id=1, source_target_pairs={{0,16},{16,0},{1,17},{17,1},{2,18},{18,2},{3,19},{19,3},{4,20},{20... | collective-permute-start | bytes 3145736 | tf_op jit(solution)/shard_map/ppermute | solution.py:19
  434.6 44.6 %collective-permute-start.4 = (bf16[512,1024]{0,1:T(8,128)(2,1)S(1)}, bf16[512,1024]{0,1:T(8,128)(2,1)S(1)}, u32[]{:S(2)}, u32[]{:S(2)}) collective-permute-start(bf16[512,1024]{0,1:T(8,128)(2,1)S(1)} %slice.87), channel_id=1, source_target_pairs={{0,16},{16,0},{1,17},{17,1},{2,18},{18,2},{3,19},{19,3},{4,20},{20... | collective-permute-start | bytes 3145736 | tf_op jit(solution)/shard_map/ppermute | solution.py:19
  502.3 316.3 %reduce-scatter.9.cloned.1.call-start = ((), (), s32[]{:S(2)}) async-start(), calls=%async_computation.9 | async-start | bytes 17825792 | tf_op jit(solution)/shard_map/reduce_scatter | solution.py:286
  516.6 484.3 %reduce-scatter.11.cloned.1.call-start = ((), (), s32[]{:S(2)}) async-start(), calls=%async_computation.10 | async-start | bytes 17825792 | tf_op jit(solution)/shard_map/reduce_scatter | solution.py:288
  529.8 555.1 %all-reduce.21.cloned.1.call-start = ((), (), s32[]{:S(2)}) async-start(), calls=%async_computation.12 | async-start | bytes 3932160 | tf_op jit(solution)/shard_map/psum | solution.py:294
  638.6 368.6 %copy-start.30 = (f32[1024]{0:T(1024)S(1)}, f32[1024]{0:T(1024)}, u32[]{:S(2)}) copy-start(f32[1024]{0:T(1024)} %get-tuple-element.462) | copy-start | bytes 12292
  638.6 368.6 %copy-start.31 = (f32[1024]{0:T(1024)S(1)}, f32[1024]{0:T(1024)}, u32[]{:S(2)}) copy-start(f32[1024]{0:T(1024)} %get-tuple-element.467) | copy-start | bytes 12292
  638.6 368.6 %copy-start.32 = (f32[1024]{0:T(1024)S(1)}, f32[1024]{0:T(1024)}, u32[]{:S(2)}) copy-start(f32[1024]{0:T(1024)} %get-tuple-element.535) | copy-start | bytes 12292
  638.6 368.6 %copy-start.33 = (f32[4096]{0:T(1024)S(1)}, f32[4096]{0:T(1024)}, u32[]{:S(2)}) copy-start(f32[4096]{0:T(1024)} %get-tuple-element.576) | copy-start | bytes 49156
  638.6 368.6 %copy-start.35 = (f32[1024]{0:T(1024)S(1)}, f32[1024]{0:T(1024)}, u32[]{:S(2)}) copy-start(f32[1024]{0:T(1024)} %get-tuple-element.533) | copy-start | bytes 12292
  638.6 368.6 %copy-start.41 = (f32[1024]{0:T(1024)S(1)}, f32[1024]{0:T(1024)}, u32[]{:S(2)}) copy-start(f32[1024]{0:T(1024)} %get-tuple-element.460) | copy-start | bytes 12292
  638.6 368.6 %copy-start.42 = (f32[1024]{0:T(1024)S(1)}, f32[1024]{0:T(1024)}, u32[]{:S(2)}) copy-start(f32[1024]{0:T(1024)} %get-tuple-element.465) | copy-start | bytes 12292
  638.6 438.1 %copy-start.10 = (f32[512,1024]{1,0:T(8,128)S(1)}, f32[512,1024]{1,0:T(8,128)}, u32[]{:S(2)}) copy-start(f32[512,1024]{1,0:T(8,128)} %copy-done.9) | copy-start | bytes 6291460
  (60 other events, 626.0 us)
Sparse Core Ops, SparseCore 0:
  11.0 65.0 all-gather.5
  78.8 40.0 all-gather.7
  121.7 73.6 all-gather.9
  197.4 73.1 all-gather.11
  318.3 71.1 reduce-scatter.6
  502.5 133.7 reduce-scatter.12
  640.9 177.6 reduce-scatter.8
  823.3 177.5 reduce-scatter.10
  1004.1 59.5 all-reduce.20
where the time goes:
time: 1110 us; the launch traced here: 1100 us
  waiting for transfers between devices  519 us (47%)
  matrix products  211 us (19%)
  blocking collectives  147 us (13%)
  local copies, waits for them, and re-layouts  118 us (11%)
  other arithmetic  78.1 us (7%)
  between operations  18.1 us (2%)
    reduce_scatter x1, waiting for transfers between devices, local(): lax.psum_scatter(down_w_grad, 'shard', scatter_dimension=0, tiled=True)  180 us
    reduce_scatter x1, waiting for transfers between devices, local(): lax.psum_scatter(up_w_grad, 'shard', scatter_dimension=0, tiled=True)  180 us
    unnamed x2, blocking collectives  124 us
    unnamed x10, waiting for transfers between devices  105 us
    ppermute x5, waiting for transfers between devices, from_partner(): return lax.ppermute(value, axis, pairs)  52.6 us
    unnamed x130, local copies, waits for them, and re-layouts  37.7 us
    dot_general x1, matrix products, local(): jnp.dot(first_low, up_w, preferred_element_type=f32) + up_b.astype(f32)  28.1 us
    dot_general x8, matrix products, masked_scores(): jnp.einsum('thd,khd->htk', q_part, k_part, preferred_element_type=f32)  25.1 us
  transfers between devices with their start and end apart: 14, of which 7 were waited for; matrix products, arithmetic and copies ran while one was open for 29% of the time, Pallas kernels for 0%

commit v1 on v0

v1 whole, which is shorter than its diff:
```python
import functools
import math

import jax
import jax.numpy as jnp
from jax import lax
from jax.experimental import pallas as pl
from jax.experimental.pallas import tpu as pltpu
from jax.sharding import PartitionSpec as P

D = 1024
HEADS = 16
HEAD_DIM = 64
FF = 4096
SLABS = 12
LANES = 128
MASKED = -1e30
MESH = pl.DeviceIdType.MESH
VMEM = 60 * 1024 * 1024
BF = jnp.bfloat16
F32 = jnp.float32

ERFC_P = 0.33
ERFC_Q = (
    0.1863661,
    0.182837329,
    0.20192357,
    0.0450108379,
    0.412542064,
    -0.355440048,
    0.462689118,
    -0.135929052,
)


def dot(a, b):
    return lax.dot_general(a, b, (((1,), (0,)), ((), ())), preferred_element_type=F32)


def dot_nt(a, b):
    return lax.dot_general(a, b, (((1,), (1,)), ((), ())), preferred_element_type=F32)


def dot_tn(a, b):
    return lax.dot_general(a, b, (((0,), (0,)), ((), ())), preferred_element_type=F32)


def swap_halves(a):
    width = a.shape[1]
    lane = lax.broadcasted_iota(jnp.int32, a.shape, 1) % HEAD_DIM
    return jnp.where(
        lane < HEAD_DIM // 2,
        pltpu.roll(a, width - HEAD_DIM // 2, 1),
        pltpu.roll(a, HEAD_DIM // 2, 1),
    )


def split3(a):
    hi = a.astype(BF)
    rest = a - hi.astype(F32)
    mid = rest.astype(BF)
    low = (rest - mid.astype(F32)).astype(BF)
    return hi, mid, low


def swap_width(slab):
    return 384 if slab % 2 == 0 else 256


def remote(src, dst, send, recv, device):
    return pltpu.make_async_remote_copy(
        src_ref=src, dst_ref=dst, send_sem=send, recv_sem=recv, device_id=device, device_id_type=MESH
    )


def place(hi_count):
    index = lax.axis_index("shard")
    return index // 4, (index // 2) % 2, index % 2, lax.axis_index("rep")


def shard_of(hi, mid, core):
    return {"shard": hi * 4 + mid * 2 + core}


def entry_barrier(hi_count, hi, mid, core, rep):
    barrier = pltpu.get_barrier_semaphore()
    for m in range(1, hi_count):
        pl.semaphore_signal(
            barrier, inc=1, device_id=shard_of((hi + m) % hi_count, mid, core), device_id_type=MESH
        )
    pl.semaphore_signal(barrier, inc=1, device_id=shard_of(hi, 1 - mid, core), device_id_type=MESH)
    pl.semaphore_signal(barrier, inc=1, device_id=shard_of(hi, mid, 1 - core), device_id_type=MESH)
    pl.semaphore_signal(barrier, inc=1, device_id={"rep": 1 - rep}, device_id_type=MESH)
    pl.semaphore_wait(barrier, hi_count + 2)


SWAP = 256
PARTS = 2


class Gather:
    def __init__(self, hi_count, packed, full, sems, swap=SWAP):
        self.hi_count = hi_count
        self.packed, self.full = packed, full
        (self.up_send, self.up_recv, self.down_send, self.down_recv, self.y_send, self.y_recv,
         self.x_send, self.x_recv, self.c_send, self.c_recv) = sems
        self.hi, self.mid, self.core, self.rep = place(hi_count)
        slabs, self.depth, width = packed.shape
        self.parts = self.parts_of(self.depth, swap)
        self.rows = self.depth // self.parts
        self.count = slabs * self.parts
        self.swap = swap
        self.mine = slice(None)
        if swap:
            self.mine = pl.ds(pl.multiple_of(self.rep * swap, LANES), width - swap)

    @staticmethod
    def parts_of(depth, swap):
        return PARTS if swap and depth % (16 * PARTS) == 0 else 1

    @staticmethod
    def scratch(hi_count, slabs, depth, swap=SWAP):
        count = slabs * Gather.parts_of(depth, swap)
        dma = pltpu.SemaphoreType.DMA
        hops = dma((count, hi_count - 1))
        return [hops] * 4 + [dma((count,))] * 4 + [dma((count, 2))] * 2

    def only(self, which):
        return pl.ds(pl.multiple_of(which * (D - self.swap), LANES), self.swap)

    def spot(self, chunk):
        start = (chunk % self.parts) * self.rows
        if not isinstance(start, int):
            start = pl.multiple_of(start, self.rows)
        return chunk // self.parts, pl.ds(start, self.rows)

    def hop(self, chunk, distance, up):
        slab, rows = self.spot(chunk)
        origin = self.hi - distance if up else self.hi + distance
        block = self.full.at[slab, origin, self.mid, self.core, rows, self.mine]
        source = self.packed.at[slab, rows, self.mine] if distance == 0 else block
        send, recv = (self.up_send, self.up_recv) if up else (self.down_send, self.down_recv)
        device = shard_of(self.hi + 1 if up else self.hi - 1, self.mid, self.core)
        return remote(source, block, send.at[chunk, distance], recv.at[chunk, distance], device)

    def landed_hop(self, chunk, distance, up):
        slab, rows = self.spot(chunk)
        origin = self.hi - distance - 1 if up else self.hi + distance + 1
        block = self.full.at[slab, origin, self.mid, self.core, rows, self.mine]
        send, recv = (self.up_send, self.up_recv) if up else (self.down_send, self.down_recv)
        device = shard_of(self.hi, self.mid, self.core)
        return remote(block, block, send.at[chunk, distance], recv.at[chunk, distance], device)

    def sends(self, distance, up):
        if up:
            return (self.hi - distance >= 0) & (self.hi + 1 < self.hi_count)
        return (self.hi + distance < self.hi_count) & (self.hi - 1 >= 0)

    def lands(self, distance, up):
        if up:
            return self.hi - distance - 1 >= 0
        return self.hi + distance + 1 < self.hi_count

    def y_copy(self, chunk, landed):
        slab, rows = self.spot(chunk)
        which = 1 - self.mid if landed else self.mid
        block = self.full.at[slab, :, which, self.core, rows, self.mine]
        device = shard_of(self.hi, 1 - self.mid, self.core)
        return remote(block, block, self.y_send.at[chunk], self.y_recv.at[chunk], device)

    def x_copy(self, chunk, landed):
        slab, rows = self.spot(chunk)
        columns = self.only(1 - self.rep if landed else self.rep)
        block = self.full.at[slab, :, :, self.core, rows, columns]
        return remote(block, block, self.x_send.at[chunk], self.x_recv.at[chunk], {"rep": 1 - self.rep})

    def c_copy(self, chunk, part, landed):
        slab, rows = self.spot(chunk)
        which = 1 - self.core if landed else self.core
        columns = self.mine if part == 0 else self.only(1 - self.rep)
        block = self.full.at[slab, :, :, which, rows, columns]
        device = shard_of(self.hi, self.mid, 1 - self.core)
        return remote(block, block, self.c_send.at[chunk, part], self.c_recv.at[chunk, part], device)

    @property
    def lag(self):
        return self.hi_count + 2

    def own_copy(self, sem):
        target = self.full.at[:, self.hi, self.mid, self.core, :, self.mine]
        return pltpu.make_async_copy(self.packed.at[:, :, self.mine], target, sem)

    def tick(self, t):
        def stage(offset, act):
            if not isinstance(t, int):
                act(t - offset)
            elif 0 <= t - offset < self.count:
                act(t - offset)

        def own(chunk):
            for up in (True, False):
                pl.when(self.sends(0, up))(lambda: self.hop(chunk, 0, up).start())

        def forward(distance, chunk):
            for up in (True, False):
                pl.when(self.lands(distance - 1, up))(
                    lambda: self.landed_hop(chunk, distance - 1, up).wait_recv()
                )
                if distance < self.hi_count - 1:
                    pl.when(self.sends(distance, up))(lambda: self.hop(chunk, distance, up).start())
            if distance == self.hi_count - 1:
                self.y_copy(chunk, False).start()

        def after_y(chunk):
            self.y_copy(chunk, True).wait_recv()
            if self.swap:
                self.x_copy(chunk, False).start()
            self.c_copy(chunk, 0, False).start()

        def after_x(chunk):
            if self.swap:
                self.x_copy(chunk, True).wait_recv()
                self.c_copy(chunk, 1, False).start()

        def after_c(chunk):
            for part in range(2 if self.swap else 1):
                self.c_copy(chunk, part, True).wait_recv()

        stage(0, own)
        for distance in range(1, self.hi_count):
            stage(distance, functools.partial(forward, distance))
        stage(self.hi_count, after_y)
        stage(self.hi_count + 1, after_x)
        stage(self.hi_count + 2, after_c)

    def drain(self):
        @pl.loop(0, self.count)
        def _(chunk):
            for distance in range(self.hi_count - 1):
                for up in (True, False):
                    pl.when(self.sends(distance, up))(
                        lambda: self.hop(chunk, distance, up).wait_send()
                    )
            self.y_copy(chunk, False).wait_send()
            if self.swap:
                self.x_copy(chunk, False).wait_send()
            for part in range(2 if self.swap else 1):
                self.c_copy(chunk, part, False).wait_send()


def near_barrier(hi_count):
    hi, mid, core, rep = place(hi_count)
    barrier = pltpu.get_barrier_semaphore()

    def greet(device):
        pl.semaphore_signal(barrier, inc=1, device_id=device, device_id_type=MESH)

    pl.when(hi + 1 < hi_count)(lambda: greet(shard_of(hi + 1, mid, core)))
    pl.when(hi - 1 >= 0)(lambda: greet(shard_of(hi - 1, mid, core)))
    greet(shard_of(hi, 1 - mid, core))
    greet(shard_of(hi, mid, 1 - core))
    greet({"rep": 1 - rep})
    first, last = hi == 0, hi == hi_count - 1
    pl.semaphore_wait(barrier, 5 - first.astype(jnp.int32) - last.astype(jnp.int32))


def gather_kernel(hi_count, packed, vec, tokens, full, vec_full, tokens_all, local_sem, t_sem, *sems):
    rep = lax.axis_index("rep")
    gather = Gather(hi_count, packed, full, sems[:10])
    small = Gather(hi_count, vec, vec_full, sems[10:], swap=0)
    near_barrier(hi_count)
    token_copy = remote(tokens, tokens_all.at[1], t_sem.at[0], t_sem.at[1], {"rep": 1 - rep})
    token_copy.start()
    copies = [
        pltpu.make_async_copy(tokens, tokens_all.at[0], local_sem.at[0]),
        small.own_copy(local_sem.at[1]),
        gather.own_copy(local_sem.at[2]),
    ]
    for copy in copies:
        copy.start()
    for copy in copies:
        copy.wait()
    for t in range(gather.lag + 1):
        small.tick(t)
        gather.tick(t)

    @pl.loop(gather.lag + 1, gather.count)
    def _(t):
        gather.tick(t)

    for t in range(gather.count, gather.count + gather.lag):
        gather.tick(t)
    token_copy.wait()
    small.drain()
    gather.drain()


def gather(hi_count, packed, vec, tokens):
    rows = packed.shape[1]
    anywhere = pl.BlockSpec(memory_space=pl.ANY)
    return pl.pallas_call(
        functools.partial(gather_kernel, hi_count),
        out_shape=(
            jax.ShapeDtypeStruct((SLABS, hi_count, 2, 2, rows, D), BF),
            jax.ShapeDtypeStruct((1, hi_count, 2, 2) + vec.shape, BF),
            jax.ShapeDtypeStruct((2,) + tokens.shape, BF),
        ),
        in_specs=[pl.BlockSpec(memory_space=pltpu.VMEM)] * 3,
        out_specs=(anywhere,) * 3,
        scratch_shapes=[pltpu.SemaphoreType.DMA((3,)), pltpu.SemaphoreType.DMA((2,))]
        + Gather.scratch(hi_count, SLABS, rows)
        + Gather.scratch(hi_count, 1, vec.shape[0], swap=0),
        compiler_params=pltpu.CompilerParams(collective_id=0, has_side_effects=True),
        name="gather",
    )(packed, vec[None], tokens)


def scatter_kernel(
    hi_count,
    g_qkv,
    g_out,
    g_up,
    g_down,
    g_vec,
    total,
    vec_total,
    held,
    from_core,
    from_x,
    from_y,
    from_z,
    own,
    other,
    v_held,
    v_core,
    v_y,
    v_z,
    v_own,
    v_other,
    load_sem,
    c_send,
    c_recv,
    x_send,
    x_recv,
    y_send,
    y_recv,
    z_send,
    z_recv,
    f_send,
    f_recv,
):
    hi, mid, core, rep = place(hi_count)
    own[...] = jnp.zeros_like(own)
    other[...] = jnp.zeros_like(other)
    entry_barrier(hi_count, hi, mid, core, rep)
    sent = []

    def source(slab, which):
        if slab < 3:
            return g_qkv.at[:, :, which, :, slab * D : (slab + 1) * D]
        if slab == 3:
            return g_out.at[:, :, which]
        if slab < 8:
            return g_up.at[:, :, which, :, (slab - 4) * D : (slab - 3) * D]
        if slab < SLABS:
            return g_down.at[slab - 8, :, :, which]
        return g_vec.at[:, :, which]

    def c_copy(slab):
        land = from_core.at[slab] if slab < SLABS else v_core
        return remote(
            source(slab, 1 - core),
            land,
            c_send.at[slab],
            c_recv.at[slab],
            shard_of(hi, mid, 1 - core),
        )

    def load(slab):
        land = held.at[slab] if slab < SLABS else v_held
        return pltpu.make_async_copy(source(slab, core), land, load_sem.at[slab])

    def mine(slab):
        width = D - swap_width(slab)
        return pl.ds(pl.multiple_of(rep * swap_width(slab), LANES), width)

    def only(slab, which):
        width = swap_width(slab)
        return pl.ds(pl.multiple_of(which * (D - width), LANES), width)

    def x_copy(slab):
        width = swap_width(slab)
        return remote(
            held.at[slab, :, :, :, only(slab, 1 - rep)],
            from_x.at[slab, :, :, :, :width],
            x_send.at[slab],
            x_recv.at[slab],
            {"rep": 1 - rep},
        )

    def y_copy(slab):
        if slab < SLABS:
            width = D - swap_width(slab)
            src = held.at[slab, :, 1 - mid, :, mine(slab)]
            dst = from_y.at[slab, :, :, :width]
        else:
            src, dst = v_held.at[:, 1 - mid], v_y
        return remote(src, dst, y_send.at[slab], y_recv.at[slab], shard_of(hi, 1 - mid, core))

    def z_copy(slab, m):
        there = (hi + m) % hi_count
        if slab < SLABS:
            width = D - swap_width(slab)
            src = held.at[slab, there, mid, :, mine(slab)]
            dst = from_z.at[slab, m - 1, :, :width]
        else:
            src, dst = v_held.at[there, mid], v_z.at[m - 1]
        return remote(
            src, dst, z_send.at[slab, m - 1], z_recv.at[slab, m - 1], shard_of(there, mid, core)
        )

    def f_copy(slab):
        if slab < SLABS:
            src, dst = own.at[slab, :, mine(slab)], other.at[slab, :, mine(slab)]
        else:
            src, dst = v_own, v_other
        return remote(src, dst, f_send.at[slab], f_recv.at[slab], {"rep": 1 - rep})

    def f_land(slab):
        if slab < SLABS:
            width = D - swap_width(slab)
            columns = pl.ds(pl.multiple_of((1 - rep) * swap_width(slab), LANES), width)
            dst = other.at[slab, :, columns]
        else:
            dst = v_other
        return remote(dst, dst, f_send.at[slab], f_recv.at[slab], {"rep": 1 - rep})

    def start(copy):
        copy.start()
        sent.append(copy)

    def add_core(slab):
        if slab == SLABS:
            v_held[...] += v_core[...]
            return

        @pl.loop(0, hi_count)
        def _(h):
            for m in range(2):
                held[slab, h, m] = (
                    held[slab, h, m].astype(F32) + from_core[slab, h, m].astype(F32)
                ).astype(BF)

    def add_x(slab):
        width = swap_width(slab)

        @pl.loop(0, hi_count)
        def _(h):
            for m in range(2):
                held[slab, h, m, :, only(slab, rep)] = (
                    held[slab, h, m, :, only(slab, rep)].astype(F32)
                    + from_x[slab, h, m, :, :width].astype(F32)
                ).astype(BF)

    def add_y(slab):
        if slab == SLABS:
            v_held[:, mid] += v_y[...]
            return
        width = D - swap_width(slab)

        @pl.loop(0, hi_count)
        def _(h):
            held[slab, h, mid, :, mine(slab)] = (
                held[slab, h, mid, :, mine(slab)].astype(F32)
                + from_y[slab, h, :, :width].astype(F32)
            ).astype(BF)

    def add_z(slab):
        if slab == SLABS:
            v_own[...] = v_held[hi, mid] + jnp.sum(v_z[...], axis=0)
            return
        width = D - swap_width(slab)
        value = held[slab, hi, mid, :, mine(slab)].astype(F32)
        for m in range(hi_count - 1):
            value += from_z[slab, m, :, :width].astype(F32)
        own[slab, :, mine(slab)] = value.astype(BF)

    order = [8, 9, 10, 11, 4, 5, 6, 7, 3, 0, 1, 2, SLABS]
    count = len(order)
    for slab in order:
        start(c_copy(slab))
        load(slab).start()
    for tick in range(count + 4):
        if tick < count:
            slab = order[tick]
            c_copy(slab).wait_recv()
            load(slab).wait()
            add_core(slab)
            if slab < SLABS:
                start(x_copy(slab))
        if 0 <= tick - 1 < count:
            slab = order[tick - 1]
            if slab < SLABS:
                x_copy(slab).wait_recv()
                add_x(slab)
            start(y_copy(slab))
        if 0 <= tick - 2 < count:
            slab = order[tick - 2]
            y_copy(slab).wait_recv()
            add_y(slab)
            for m in range(1, hi_count):
                start(z_copy(slab, m))
        if 0 <= tick - 3 < count:
            slab = order[tick - 3]
            for m in range(1, hi_count):
                z_copy(slab, m).wait_recv()
            add_z(slab)
            start(f_copy(slab))
        if 0 <= tick - 4 < count:
            slab = order[tick - 4]
            f_land(slab).wait_recv()
            if slab < SLABS:
                total[slab] = own[slab].astype(F32) + other[slab].astype(F32)
            else:
                vec_total[...] = v_own[...] + v_other[...]
    for copy in sent:
        copy.wait_send()


def scatter(hi_count, g_qkv, g_out, g_up, g_down, g_vec):
    rows = D // (4 * hi_count)
    dma = pltpu.SemaphoreType.DMA
    anywhere = pl.BlockSpec(memory_space=pl.ANY)
    vmem = pl.BlockSpec(memory_space=pltpu.VMEM)
    most, least = D - swap_width(1), swap_width(0)
    vec = g_vec.shape[1:]

    def blocks(a):
        return a.reshape((hi_count, 2, 2, rows, a.shape[-1]))

    return pl.pallas_call(
        functools.partial(scatter_kernel, hi_count),
        out_shape=(
            jax.ShapeDtypeStruct((SLABS, rows, D), F32),
            jax.ShapeDtypeStruct(vec, F32),
        ),
        in_specs=[anywhere] * 5,
        out_specs=(vmem,) * 2,
        scratch_shapes=[
            pltpu.VMEM((SLABS, hi_count, 2, rows, D), BF),
            pltpu.VMEM((SLABS, hi_count, 2, rows, D), BF),
            pltpu.VMEM((SLABS, hi_count, 2, rows, least), BF),
            pltpu.VMEM((SLABS, hi_count, rows, most), BF),
            pltpu.VMEM((SLABS, hi_count - 1, rows, most), BF),
            pltpu.VMEM((SLABS, rows, D), BF),
            pltpu.VMEM((SLABS, rows, D), BF),
            pltpu.VMEM((hi_count, 2) + vec, F32),
            pltpu.VMEM((hi_count, 2) + vec, F32),
            pltpu.VMEM((hi_count,) + vec, F32),
            pltpu.VMEM((hi_count - 1,) + vec, F32),
            pltpu.VMEM(vec, F32),
            pltpu.VMEM(vec, F32),
            dma((SLABS + 1,)),
            dma((SLABS + 1,)),
            dma((SLABS + 1,)),
            dma((SLABS + 1,)),
            dma((SLABS + 1,)),
            dma((SLABS + 1,)),
            dma((SLABS + 1,)),
            dma((SLABS + 1, hi_count - 1)),
            dma((SLABS + 1, hi_count - 1)),
            dma((SLABS + 1,)),
            dma((SLABS + 1,)),
        ],
        compiler_params=pltpu.CompilerParams(
            collective_id=1, has_side_effects=True, vmem_limit_bytes=VMEM
        ),
        name="scatter",
    )(
        blocks(g_qkv),
        blocks(g_out),
        blocks(g_up),
        g_down.reshape(4, hi_count, 2, 2, rows, D),
        g_vec.reshape((hi_count, 2, 2) + vec),
    )


QUAD = 4 * HEAD_DIM


def attend_kernel(
    tokens, w_q, w_k, w_v, bias, cosine, sine, q_doc, k_doc, q_out, k_out, v_out, context, q_ext
):
    own_rows = q_out.shape[0]
    x = tokens[...]
    cos_all = jnp.concatenate([cosine[...], cosine[...]], axis=1)
    sin_all = jnp.concatenate([sine[...], sine[...]], axis=1)

    def rope(a, count):
        return a * cos_all[:count] + swap_halves(a) * sin_all[:count]

    q_rows = rope(dot(x[:own_rows], w_q[0]) + bias[0:1], own_rows) * HEAD_DIM**-0.5
    q_out[...] = q_rows.astype(BF)
    k_out[...] = rope(dot(x, w_k[0]) + bias[1:2], 2 * own_rows).astype(BF)
    v_out[...] = (dot(x, w_v[0]) + bias[2:3]).astype(BF)
    doc_k = k_doc[...]
    ones = jnp.ones((2 * own_rows, LANES), BF)
    piece = 256
    for pair in range(2):
        lanes = slice(pair * LANES, (pair + 1) * LANES)
        keys = jnp.concatenate([k_out[:, lanes], doc_k], axis=1)
        values = jnp.concatenate([v_out[:, lanes], ones], axis=1)
        for start in range(0, own_rows, piece):
            rows = slice(start, start + piece)
            q_pair = q_out[rows, lanes]
            lane = lax.broadcasted_iota(jnp.int32, q_pair.shape, 1)
            doc_q = q_doc[rows, :]
            mixed = []
            for head in range(2):
                in_head = (lane // HEAD_DIM) == head
                queries = jnp.concatenate([jnp.where(in_head, q_pair, 0), doc_q], axis=1)
                scores = dot_nt(queries, keys)
                row_max = jnp.max(scores, axis=1, keepdims=True)
                prob = jnp.exp(scores - row_max).astype(BF)
                both = dot(prob, values)
                row_sum = both[:, LANES:]
                mixed.append(both[:, :LANES] / row_sum)
                log_total = row_max + jnp.log(row_sum)
                hi, mid, low = split3(-log_total)
                ext = jnp.where(lane == 61, hi, doc_q)
                ext = jnp.where(lane == 62, mid, ext)
                ext = jnp.where(lane == 63, low, ext)
                q_ext[pair * 2 + head, rows, :] = ext
            context[rows, lanes] = jnp.where(lane < HEAD_DIM, mixed[0], mixed[1]).astype(BF)


def attend(tokens_all, full, bias, cosine, sine, q_doc, k_doc):
    rows = tokens_all.shape[0] // 2
    whole = lambda *shape: pl.BlockSpec(shape, lambda i: (0,) * len(shape))
    weight = lambda slab: pl.BlockSpec((1, D, QUAD), lambda i: (slab, 0, i))
    columns = lambda count: pl.BlockSpec((count, QUAD), lambda i: (0, i))
    return pl.pallas_call(
        attend_kernel,
        grid=(HEADS // 4,),
        out_shape=(
            jax.ShapeDtypeStruct((rows, D), BF),
            jax.ShapeDtypeStruct((2 * rows, D), BF),
            jax.ShapeDtypeStruct((2 * rows, D), BF),
            jax.ShapeDtypeStruct((rows, D), BF),
            jax.ShapeDtypeStruct((HEADS, rows, LANES), BF),
        ),
        in_specs=[
            whole(2 * rows, D),
            weight(0),
            weight(1),
            weight(2),
            columns(3),
            whole(2 * rows, LANES),
            whole(2 * rows, LANES),
            whole(rows, LANES),
            whole(2 * rows, LANES),
        ],
        out_specs=(
            columns(rows),
            columns(2 * rows),
            columns(2 * rows),
            columns(rows),
            pl.BlockSpec((4, rows, LANES), lambda i: (i, 0, 0)),
        ),
        compiler_params=pltpu.CompilerParams(vmem_limit_bytes=VMEM),
        name="attend",
    )(tokens_all, full, full, full, bias, cosine, sine, q_doc, k_doc)


def attend_back_kernel(
    q_in, k_in, v_in, context, d_context, q_ext, k_doc, cosine, sine, d_q, d_k, d_v
):
    own_rows = q_in.shape[0]
    doc_k = k_doc[...]
    for pair in range(2):
        lanes = slice(pair * LANES, (pair + 1) * LANES)
        k_pair, v_pair = k_in[:, lanes], v_in[:, lanes]
        q_pair, g_pair = q_in[:, lanes], d_context[:, lanes]
        lane = lax.broadcasted_iota(jnp.int32, q_pair.shape, 1)
        k_lane = lax.broadcasted_iota(jnp.int32, k_pair.shape, 1)
        keys = jnp.concatenate([k_pair, doc_k], axis=1)
        minus = jnp.where(k_lane < 3, -1.0, 0.0).astype(BF)
        values = jnp.concatenate([v_pair, minus], axis=1)
        product = g_pair.astype(F32) * context[:, lanes].astype(F32)
        dq = jnp.zeros(q_pair.shape, F32)
        dk = jnp.zeros(k_pair.shape, F32)
        dv = jnp.zeros(k_pair.shape, F32)
        for head in range(2):
            in_head = (lane // HEAD_DIM) == head
            q_head = jnp.where(in_head, q_pair, 0)
            g_head = jnp.where(in_head, g_pair, 0)
            inner = jnp.sum(jnp.where(in_head, product, 0.0), axis=1, keepdims=True)
            hi, mid, low = split3(jnp.broadcast_to(inner, q_pair.shape))
            g_ext = jnp.where(lane == 0, hi, jnp.where(lane == 1, mid, low))
            g_ext = jnp.where(lane < 3, g_ext, 0)
            scores = dot_nt(keys, jnp.concatenate([q_head, q_ext[pair * 2 + head]], axis=1))
            prob = jnp.exp(scores)
            dv += dot(prob.astype(BF), g_head)
            d_prob = dot_nt(values, jnp.concatenate([g_head, g_ext], axis=1))
            d_score = (prob * d_prob).astype(BF)
            dk += dot(d_score, q_head)
            k_head = jnp.where((k_lane // HEAD_DIM) == head, k_pair, 0)
            dq += dot_tn(d_score, k_head)
        dq *= HEAD_DIM**-0.5
        cos_all, sin_all = cosine[...], sine[...]
        d_q[:, lanes] = (dq * cos_all[:own_rows] + swap_halves(dq * sin_all[:own_rows])).astype(BF)
        d_k[:, lanes] = (dk * cos_all + swap_halves(dk * sin_all)).astype(BF)
        d_v[:, lanes] = dv.astype(BF)


def attend_back(q, k, v, context, d_context, q_ext, k_doc, cosine, sine):
    rows = q.shape[0]
    whole = lambda *shape: pl.BlockSpec(shape, lambda i: (0,) * len(shape))
    columns = lambda count: pl.BlockSpec((count, QUAD), lambda i: (0, i))
    return pl.pallas_call(
        attend_back_kernel,
        grid=(HEADS // 4,),
        out_shape=(
            jax.ShapeDtypeStruct((rows, D), BF),
            jax.ShapeDtypeStruct((2 * rows, D), BF),
            jax.ShapeDtypeStruct((2 * rows, D), BF),
        ),
        in_specs=[
            columns(rows),
            columns(2 * rows),
            columns(2 * rows),
            columns(rows),
            columns(rows),
            pl.BlockSpec((4, rows, LANES), lambda i: (i, 0, 0)),
            whole(2 * rows, LANES),
            whole(2 * rows, LANES),
            whole(2 * rows, LANES),
        ],
        out_specs=(columns(rows), columns(2 * rows), columns(2 * rows)),
        compiler_params=pltpu.CompilerParams(vmem_limit_bytes=VMEM),
        name="attend_back",
    )(q, k, v, context, d_context, q_ext, k_doc, cosine, sine)


def normed_rows(residual):
    mean_val = jnp.mean(residual, axis=-1, keepdims=True)
    centred = residual - mean_val
    variance = jnp.mean(centred * centred, axis=-1, keepdims=True)
    inv_std = lax.rsqrt(variance + 1e-05)
    return centred * inv_std, inv_std


def norm_back(upstream, normed, inv_std, gain_vec):
    scaled = upstream * gain_vec
    return inv_std * (
        scaled
        - jnp.mean(scaled, axis=-1, keepdims=True)
        - normed * jnp.mean(scaled * normed, axis=-1, keepdims=True)
    )


def column_sum(a):
    return jnp.sum(a, axis=0, keepdims=True)


CHUNK = 512
CHUNKS = FF // CHUNK


def forward_kernel(
    tokens,
    context,
    w_out,
    cotangent,
    vectors,
    b_up,
    w_up,
    w_down,
    result,
    first_out,
    normed_out,
    inv_out,
    active,
    slope,
    d_second,
    d_ffn,
    sums,
    first,
    total,
):
    step = pl.program_id(0)

    @pl.when(step == 0)
    def _():
        attn = dot(context[...], w_out[0]) + vectors[0:1]
        normed, inv_std = normed_rows(tokens[0].astype(F32) + attn)
        first[...] = normed * vectors[1:2] + vectors[2:3]
        first_out[...] = first[...].astype(BF)
        normed_out[...] = normed
        inv_out[...] = jnp.broadcast_to(inv_std, inv_out.shape)

    hidden = dot(first_out[...], w_up[0]) + b_up[...]
    gauss = jnp.exp(hidden * hidden * -0.5)
    t = 1.0 / (1.0 + (ERFC_P * math.sqrt(0.5)) * jnp.abs(hidden))
    poly = jnp.full_like(t, ERFC_Q[-1])
    for coefficient in ERFC_Q[-2::-1]:
        poly = poly * t + coefficient
    tail = 0.5 * t * poly * gauss
    cdf = jnp.where(hidden >= 0, 1.0 - tail, tail)
    act = (hidden * cdf).astype(BF)
    active[...] = act
    slope[...] = (cdf + hidden * gauss * (1.0 / math.sqrt(2.0 * math.pi))).astype(slope.dtype)
    part = dot(act, w_down[0])

    @pl.when(step == 0)
    def _():
        total[...] = part

    @pl.when(step > 0)
    def _():
        total[...] += part

    @pl.when(step == CHUNKS - 1)
    def _():
        gain = vectors[4:5]
        normed, inv_std = normed_rows(first[...] + total[...] + vectors[3:4])
        result[...] = (normed * gain + vectors[5:6]).astype(BF)
        up = cotangent[...].astype(F32)
        sums[0:1] = column_sum(up * normed)
        sums[1:2] = column_sum(up)
        grad = norm_back(up, normed, inv_std, gain)
        d_second[...] = grad
        low = grad.astype(BF)
        d_ffn[...] = low
        sums[2:3] = column_sum(low.astype(F32))


def forward(tokens_all, context, full, cotangent, vectors, b_up):
    rows = context.shape[0]
    per = D // CHUNK
    whole = lambda *shape: pl.BlockSpec(shape, lambda i: (0,) * len(shape))
    wide = pl.BlockSpec((rows, CHUNK), lambda i: (0, i))
    return pl.pallas_call(
        forward_kernel,
        grid=(CHUNKS,),
        out_shape=(
            jax.ShapeDtypeStruct((rows, D), BF),
            jax.ShapeDtypeStruct((rows, D), BF),
            jax.ShapeDtypeStruct((rows, D), F32),
            jax.ShapeDtypeStruct((rows, LANES), F32),
            jax.ShapeDtypeStruct((rows, FF), BF),
            jax.ShapeDtypeStruct((rows, FF), F32),
            jax.ShapeDtypeStruct((rows, D), F32),
            jax.ShapeDtypeStruct((rows, D), BF),
            jax.ShapeDtypeStruct((3, D), F32),
        ),
        in_specs=[
            pl.BlockSpec((1, rows, D), lambda i: (0, 0, 0)),
            whole(rows, D),
            pl.BlockSpec((1, D, D), lambda i: (3, 0, 0)),
            whole(rows, D),
            whole(6, D),
            pl.BlockSpec((1, CHUNK), lambda i: (0, i)),
            pl.BlockSpec((1, D, CHUNK), lambda i: (4 + i // per, 0, i % per)),
            pl.BlockSpec((1, CHUNK, D), lambda i: (8 + i // per, i % per, 0)),
        ],
        out_specs=(
            whole(rows, D),
            whole(rows, D),
            whole(rows, D),
            whole(rows, LANES),
            wide,
            wide,
            whole(rows, D),
            whole(rows, D),
            whole(3, D),
        ),
        scratch_shapes=[pltpu.VMEM((rows, D), F32), pltpu.VMEM((rows, D), F32)],
        compiler_params=pltpu.CompilerParams(vmem_limit_bytes=VMEM),
        name="forward",
    )(tokens_all, context, full, cotangent, vectors, b_up, full, full)


def backward_kernel(
    d_ffn,
    d_second,
    first,
    normed,
    inv_std,
    context,
    vectors,
    w_out,
    active,
    slope,
    w_up,
    w_down,
    g_down,
    g_up,
    g_b_up,
    g_out,
    d_resid,
    d_context,
    sums,
    total,
):
    step = pl.program_id(0)
    low = d_ffn[...]
    d_hidden = (dot_nt(low, w_down[0]) * slope[...]).astype(BF)
    g_down[...] = dot_tn(active[...], low).astype(BF)
    g_up[...] = dot_tn(first[...], d_hidden).astype(BF)
    g_b_up[...] = column_sum(d_hidden.astype(F32))
    part = dot_nt(d_hidden, w_up[0])

    @pl.when(step == 0)
    def _():
        total[...] = d_second[...] + part

    @pl.when(step > 0)
    def _():
        total[...] += part

    @pl.when(step == CHUNKS - 1)
    def _():
        up = total[...]
        sums[0:1] = column_sum(up * normed[...])
        sums[1:2] = column_sum(up)
        grad = norm_back(up, normed[...], inv_std[:, 0:1], vectors[1:2])
        d_resid[...] = grad
        d_attn = grad.astype(BF)
        sums[2:3] = column_sum(d_attn.astype(F32))
        g_out[...] = dot_tn(context[...], d_attn).astype(BF)
        d_context[...] = dot_nt(d_attn, w_out[0]).astype(BF)


def backward(d_ffn, d_second, first, normed, inv_std, context, vectors, full, active, slope):
    rows = context.shape[0]
    per = D // CHUNK
    whole = lambda *shape: pl.BlockSpec(shape, lambda i: (0,) * len(shape))
    wide = pl.BlockSpec((rows, CHUNK), lambda i: (0, i))
    return pl.pallas_call(
        backward_kernel,
        grid=(CHUNKS,),
        out_shape=(
            jax.ShapeDtypeStruct((FF, D), BF),
            jax.ShapeDtypeStruct((D, FF), BF),
            jax.ShapeDtypeStruct((1, FF), F32),
            jax.ShapeDtypeStruct((D, D), BF),
            jax.ShapeDtypeStruct((rows, D), F32),
            jax.ShapeDtypeStruct((rows, D), BF),
            jax.ShapeDtypeStruct((3, D), F32),
        ),
        in_specs=[
            whole(rows, D),
            whole(rows, D),
            whole(rows, D),
            whole(rows, D),
            whole(rows, LANES),
            whole(rows, D),
            whole(6, D),
            pl.BlockSpec((1, D, D), lambda i: (3, 0, 0)),
            wide,
            wide,
            pl.BlockSpec((1, D, CHUNK), lambda i: (4 + i // per, 0, i % per)),
            pl.BlockSpec((1, CHUNK, D), lambda i: (8 + i // per, i % per, 0)),
        ],
        out_specs=(
            pl.BlockSpec((CHUNK, D), lambda i: (i, 0)),
            pl.BlockSpec((D, CHUNK), lambda i: (0, i)),
            pl.BlockSpec((1, CHUNK), lambda i: (0, i)),
            whole(D, D),
            whole(rows, D),
            whole(rows, D),
            whole(3, D),
        ),
        scratch_shapes=[pltpu.VMEM((rows, D), F32)],
        compiler_params=pltpu.CompilerParams(vmem_limit_bytes=VMEM),
        name="backward",
    )(d_ffn, d_second, first, normed, inv_std, context, vectors, full, active, slope, full, full)


def project_back_kernel(tokens, d_joined, d_resid, weight, g_qkv, g_bias, input_grad):
    step = pl.program_id(0)
    low = d_joined[...]
    g_qkv[...] = dot_tn(tokens[0], low).astype(BF)
    g_bias[...] = column_sum(low.astype(F32))
    part = dot_nt(low, weight[0])

    @pl.when(step == 0)
    def _():
        input_grad[...] = d_resid[...] + part

    @pl.when(step > 0)
    def _():
        input_grad[...] += part


def project_back(tokens_all, d_joined, d_resid, full):
    rows = d_joined.shape[0]
    per = D // CHUNK
    whole = lambda *shape: pl.BlockSpec(shape, lambda i: (0,) * len(shape))
    return pl.pallas_call(
        project_back_kernel,
        grid=(3 * per,),
        out_shape=(
            jax.ShapeDtypeStruct((D, 3 * D), BF),
            jax.ShapeDtypeStruct((1, 3 * D), F32),
            jax.ShapeDtypeStruct((rows, D), F32),
        ),
        in_specs=[
            pl.BlockSpec((1, rows, D), lambda i: (0, 0, 0)),
            pl.BlockSpec((rows, CHUNK), lambda i: (0, i)),
            whole(rows, D),
            pl.BlockSpec((1, D, CHUNK), lambda i: (i // per, 0, i % per)),
        ],
        out_specs=(
            pl.BlockSpec((D, CHUNK), lambda i: (0, i)),
            pl.BlockSpec((1, CHUNK), lambda i: (0, i)),
            whole(rows, D),
        ),
        compiler_params=pltpu.CompilerParams(vmem_limit_bytes=VMEM),
        name="project_back",
    )(tokens_all, d_joined, d_resid, full)


def rope_tables(rows):
    half = lax.axis_index("rep")
    index = jnp.arange(2 * rows, dtype=jnp.int32)
    position = ((index + half * rows) % (2 * rows)).astype(F32)
    frequency = jnp.exp(
        jnp.arange(HEAD_DIM // 2, dtype=F32) * (-2.0 * math.log(10000.0) / HEAD_DIM)
    )
    angles = position[:, None] * frequency[None, :]
    cosine, sine = jnp.cos(angles), jnp.sin(angles)
    return (
        jnp.concatenate([cosine] * 4, axis=1),
        jnp.concatenate([-sine, sine, -sine, sine], axis=1),
    )


def local(
    tokens,
    segments,
    cotangent,
    w_qkv,
    b_qkv,
    w_out,
    b_out,
    gain_one,
    shift_one,
    w_up,
    b_up,
    w_down,
    b_down,
    gain_two,
    shift_two,
):
    rows = tokens.shape[0]
    shards = lax.axis_size("shard")
    hi_count = shards // 4
    depth = D // shards
    packed = jnp.concatenate(
        [
            w_qkv.astype(BF).reshape(depth, 3, D).transpose(1, 0, 2),
            w_out.astype(BF)[None],
            w_up.astype(BF).reshape(depth, shards, 4, depth).transpose(2, 0, 1, 3).reshape(4, depth, D),
            w_down.astype(BF).reshape(4, depth, D),
        ],
        axis=0,
    )
    small = (b_qkv, b_out, gain_one, shift_one, b_up, b_down, gain_two, shift_two)
    widths = [a.shape[0] for a in small]
    flat = jnp.concatenate([a.astype(BF) for a in small])
    flat = jnp.pad(flat, (0, -flat.shape[0] % (16 * LANES)))
    full, vec_full, tokens_all = gather(hi_count, packed, flat.reshape(-1, LANES), tokens)
    full = full.reshape(SLABS, D, D)
    vec_rows = vec_full.reshape(shards, flat.shape[0]).astype(F32)
    parts = []
    at = 0
    for width in widths:
        parts.append(vec_rows[:, at : at + width])
        at += width
    bias_qkv = parts[0].reshape(3, D)
    bias_up = parts[4].reshape(shards, 4, depth).transpose(1, 0, 2).reshape(1, FF)
    vectors = jnp.stack([parts[i].reshape(D) for i in (1, 2, 3, 5, 6, 7)])

    seg_peer = lax.ppermute(segments, "rep", [(0, 1), (1, 0)])
    seg_all = jnp.concatenate([segments, seg_peer])
    lane = jnp.arange(LANES, dtype=jnp.int32)[None, :]
    q_doc = (segments[:, None] == lane).astype(BF)
    k_doc = jnp.where((seg_all[:, None] == lane) | (lane >= 64), 0.0, MASKED)
    k_doc = jnp.where((lane >= 61) & (lane < 64), 1.0, k_doc).astype(BF)
    cosine, sine = rope_tables(rows)
    both = tokens_all.reshape(2 * rows, D)
    q, k, v, context, q_ext = attend(both, full, bias_qkv, cosine, sine, q_doc, k_doc)
    result, first, normed, inv_std, active, slope, d_second, d_ffn, sums_two = forward(
        tokens_all, context, full, cotangent, vectors, bias_up
    )
    g_down, g_up, g_b_up, g_out, d_resid, d_context, sums_one = backward(
        d_ffn, d_second, first, normed, inv_std, context, vectors, full, active, slope
    )
    d_q, d_k, d_v = attend_back(q, k, v, context, d_context, q_ext, k_doc, cosine, sine)
    peer = lax.ppermute(
        jnp.concatenate([d_k[rows:], d_v[rows:]], axis=1), "rep", [(0, 1), (1, 0)]
    ).astype(F32)
    own = jnp.concatenate([d_k[:rows], d_v[:rows]], axis=1).astype(F32)
    d_joined = jnp.concatenate([d_q, (own + peer).astype(BF)], axis=1)
    g_qkv, g_b_qkv, input_grad = project_back(tokens_all, d_joined, d_resid, full)

    g_b_up = g_b_up.reshape(4, shards, depth).transpose(1, 0, 2)
    g_small = (
        g_b_qkv,
        sums_one[2],
        sums_one[0],
        sums_one[1],
        g_b_up,
        sums_two[2],
        sums_two[0],
        sums_two[1],
    )
    g_vec = jnp.concatenate([a.reshape(shards, -1) for a in g_small], axis=1)
    g_vec = jnp.pad(g_vec, ((0, 0), (0, -g_vec.shape[1] % (8 * LANES))))
    total, vec_total = scatter(
        hi_count, g_qkv, g_out, g_up, g_down, g_vec.reshape(shards, -1, LANES)
    )
    vec_total = vec_total.reshape(-1)
    outs = []
    at = 0
    for width in widths:
        outs.append(vec_total[at : at + width])
        at += width
    grad_qkv = total[0:3].transpose(1, 0, 2).reshape(depth, 3 * D)
    grad_up = total[4:8].reshape(4, depth, shards, depth).transpose(1, 2, 0, 3).reshape(depth, FF)
    grad_down = total[8:12].reshape(4 * depth, D)
    return (
        result,
        input_grad,
        grad_qkv,
        outs[0],
        total[3],
        outs[1],
        outs[2],
        outs[3],
        grad_up,
        outs[4],
        grad_down,
        outs[5],
        outs[6],
        outs[7],
    )


def solution(mesh):
    act = P(("shard", "rep"), None)
    matrix = P("shard", None)
    vector = P("shard")
    params = (matrix, vector, matrix, vector, vector, vector, matrix, vector, matrix, vector, vector, vector)
    return jax.shard_map(
        local,
        mesh=mesh,
        in_specs=(act, P(("shard", "rep")), act) + params,
        out_specs=(act, act) + params,
        check_vma=False,
    )
```

time: 1110 us -> 492 us (0.44)
  waiting for transfers between devices: 519 us -> 46.1 us
  Pallas kernels: 0 us -> 393 us
  matrix products: 211 us -> 0 us
  blocking collectives: 147 us -> 0 us
  local copies, waits for them, and re-layouts: 118 us -> 27.7 us
  other arithmetic: 78.1 us -> 16.9 us
  between operations: 18.1 us -> 1.34 us
    pallas_call x0 -> x7, Pallas kernels: none -> 393 us  [the longest x1 133 us: gather(): pl.pallas_call(functools.partial(gather_kernel, hi_count), out_shape=(jax...]
    reduce_scatter x3 -> x0, waiting for transfers between devices: 360 us -> none  [the longest x1 180 us: local(): lax.psum_scatter(down_w_grad, 'shard', scatter_dimension=0, tiled=True)]
    dot_general x40 -> x0, matrix products: 211 us -> none  [the longest x1 28.1 us: local(): jnp.dot(first_low, up_w, preferred_element_type=f32) + up_b.astype(f32)]
    unnamed x2 -> x0, blocking collectives: 124 us -> none
    unnamed x10 -> x0, waiting for transfers between devices: 105 us -> none
    unnamed x130 -> x42, local copies, waits for them, and re-layouts: 37.7 us -> 5.06 us
    convert_element_type x41 -> x15, other arithmetic: 38.8 us -> 6.28 us  [the longest x1 2.45 us: local(): d_joined = jnp.concatenate([d_q, (own + peer).astype(BF)], axis=1)]
    dynamic_slice x32 -> x0, local copies, waits for them, and re-layouts: 21.3 us -> none  [the longest x28 21.2 us: head_block(): lax.dynamic_slice_in_dim(buffer_in, column, width_cols, 1)]
  transfers between devices with their start and end apart: 14 -> 2, of which waited for: 7 -> 1; matrix products, arithmetic and copies ran while one was open for 29% -> 3% of each run, Pallas kernels for 0% -> 27%
where the time goes in v1:
time: 492 us; the launch traced here: 489 us
  Pallas kernels  393 us (80%)
  waiting for transfers between devices  46.1 us (9%)
  local copies, waits for them, and re-layouts  27.7 us (6%)
  other arithmetic  16.9 us (3%)
    pallas_call x1, Pallas kernels, gather(): pl.pallas_call(functools.partial(gather_kernel, hi_count), out_shape=(jax...  133 us
    pallas_call x1, Pallas kernels, scatter(): pl.pallas_call(functools.partial(scatter_kernel, hi_count), out_shape=(ja...  132 us
    ppermute x1, waiting for transfers between devices, local(): lax.ppermute(jnp.concatenate([d_k[rows:], d_v[rows:]], axis=1), 'rep', [(...  46.1 us
    pallas_call x1, Pallas kernels, backward(): pl.pallas_call(backward_kernel, grid=(CHUNKS,), out_shape=(jax.ShapeDtype...  33 us
    pallas_call x1, Pallas kernels, forward(): pl.pallas_call(forward_kernel, grid=(CHUNKS,), out_shape=(jax.ShapeDtypeS...  31 us
    pallas_call x1, Pallas kernels, attend_back(): pl.pallas_call(attend_back_kernel, grid=(HEADS // 4,), out_shape=(jax.Sha...  27.2 us
    pallas_call x1, Pallas kernels, attend(): pl.pallas_call(attend_kernel, grid=(HEADS // 4,), out_shape=(jax.ShapeDty...  23.4 us
    pallas_call x1, Pallas kernels, project_back(): pl.pallas_call(project_back_kernel, grid=(3 * per,), out_shape=(jax.Shape...  13.8 us
  transfers between devices with their start and end apart: 2, of which 1 were waited for; matrix products, arithmetic and copies ran while one was open for 3% of the time, Pallas kernels for 27%

profile of v1, /device:TPU:0, one launch (start us, length us, event | category | flops | bytes accessed | tf_op | source)
XLA Modules:
  0.0 488.5 jit_solution(12194108296153745093)
XLA Ops:
  0.6 3.0 collective-permute-start
  3.7 1.5 fusion.1.q_doc
  5.2 1.3 convert_element_type.70
  10.6 1.3 pad_maximum_fusion.2.packed
  11.9 132.6 %gather.1 = (bf16[12,4,2,2,64,1024]{5,4,3,2,1,0:T(8,128)(2,1)}, bf16[1,4,2,2,16,128]{5,4,3,2,1,0:T(8,128)(2,1)}, bf16[2,512,1024]{2,1,0:T(8,128)(2,1)}) custom-call(bf16[12,64,1024]{2,1,0:T(8,128)(2,1)} %pad_maximum_fusion.2.packed, bf16[1,16,128]{2,1,0:T(8,128)(2,1)} %pad_bitcast_fusion.1.vec, bf16[512,1024]{1,0:T(8,128)(2,1)} %tokens.1), custom_call_target="tpu_custom_call" | custom-call | tf_op jit(solution)/shard_map/gather/pallas_call | solution.py:301
  145.5 1.9 fusion.2
  147.4 1.9 pad_maximum_fusion.3
  152.8 23.4 %attend.1 = (bf16[512,1024]{1,0:T(8,128)(2,1)}, bf16[1024,1024]{1,0:T(8,128)(2,1)}, bf16[1024,1024]{1,0:T(8,128)(2,1)}, bf16[512,1024]{1,0:T(8,128)(2,1)}, bf16[16,512,128]{2,1,0:T(8,128)(2,1)}) custom-call(bf16[1024,1024]{1,0:T(8,128)(2,1)} %bitcast.58, bf16[12,1024,1024]{2,1,0:T(8,128)(2,1)} %bitcast.48, bf16[12,1024,1024]{2,1,0:T(8,128)(2,1)} %bitcast.49, ...), custom_call_target="tpu_custom_call" | custom-call | tf_op jit(solution)/shard_map/attend/pallas_call | solution.py:642
  176.2 31.0 %forward.1 = (bf16[512,1024]{1,0:T(8,128)(2,1)}, bf16[512,1024]{1,0:T(8,128)(2,1)}, f32[512,1024]{1,0:T(8,128)}, f32[512,128]{1,0:T(8,128)}, bf16[512,4096]{1,0:...) custom-call(bf16[2,512,1024]{2,1,0:T(8,128)(2,1)} %get-tuple-element.4, ...), custom_call_target="tpu_custom_call" | custom-call | tf_op jit(solution)/shard_map/forward/pallas_call | solution.py:843
  207.2 33.0 %backward.1 = (bf16[4096,1024]{1,0:T(8,128)(2,1)}, bf16[1024,4096]{1,0:T(8,128)(2,1)}, f32[1,4096]{1,0:T(1,128)}, bf16[1024,1024]{1,0:T(8,128)(2,1)}, f32[512,10...) custom-call(bf16[512,1024]{1,0:T(8,128)(2,1)} %get-tuple-element.54.d_ffn, ...), custom_call_target="tpu_custom_call" | custom-call | tf_op jit(solution)/shard_map/backward/pallas_call | solution.py:940
  240.2 27.2 %attend_back.1 = (bf16[512,1024]{1,0:T(8,128)(2,1)}, bf16[1024,1024]{1,0:T(8,128)(2,1)}, bf16[1024,1024]{1,0:T(8,128)(2,1)}) custom-call(bf16[512,1024]{1,0:T(8,128)(2,1)} %get-tuple-element.51.q_in, bf16[1024,1024]{1,0:T(8,128)(2,1)} %get-tuple-element.52.k_in, bf16[1024,1024]{1,0:T(8,128)(2,1)} %get-tuple-element.53.v_in, ...), custom_call_target="tpu_custom_call" | custom-call | tf_op jit(solution)/shard_map/attend_back/pallas_call | solution.py:720
  267.4 1.9 fusion.9
  269.8 1.5 pad_maximum_fusion.1
  273.9 46.1 %collective-permute-done.1 = bf16[512,2048]{1,0:T(8,128)(2,1)} collective-permute-done((bf16[512,2048]{1,0:T(8,128)(2,1)}, bf16[512,2048]{1,0:T(8,128)(2,1)}, u32[]{:S(2)}, u32[]{:S(2)}) %collective-permute-start.1) | collective-permute-done | bytes 2097184 | tf_op jit(solution)/shard_map/ppermute | solution.py:1102
  320.0 2.4 add_convert_fusion
  322.5 1.9 pad_maximum_fusion.d_joined
  324.4 13.8 %project_back.1 = (bf16[1024,3072]{1,0:T(8,128)(2,1)}, f32[1,3072]{1,0:T(1,128)}, f32[512,1024]{1,0:T(8,128)}) custom-call(bf16[2,512,1024]{2,1,0:T(8,128)(2,1)} %get-tuple-element.46.tokens, bf16[512,3072]{1,0:T(8,128)(2,1)} %pad_maximum_fusion.d_joined, f32[512,1024]{1,0:T(8,128)} %get-tuple-element.66.d_resid, bf16[12,1024,1024]{2,1,0:T(8,128)(2,1)} %bitcast.57), custom_call_target="tpu_custom_call" | custom-call | tf_op jit(solution)/shard_map/project_back/pallas_call | solution.py:1001
  338.1 1.4 reduce.30
  340.3 131.9 %scatter.1 = (f32[12,64,1024]{2,1,0:T(8,128)}, f32[8,128]{1,0:T(8,128)}) custom-call(bf16[4,2,2,64,3072]{4,3,2,1,0:T(8,128)(2,1)} %bitcast.62, bf16[4,2,2,64,1024]{4,3,2,1,0:T(8,128)(2,1)} %bitcast.64, bf16[4,2,2,64,4096]{4,3,2,1,0:T(8,128)(2,1)} %bitcast.60, bf16[4,4,2,2,64,1024]{5,4,3,2,1,0:T(8,128)(2,1)} %bitcast.59, f32[4,2,2,8,128]{4,3,2,1,0:T(8,128)} %bitcast.73), custom_call_target="tpu_custom_call" | custom-call | tf_op jit(solution)/shard_map/scatter/pallas_call | solution.py:541
  472.2 2.7 fusion.8
  474.9 2.1 slice_bitcast_fusion
  477.0 1.7 slice_bitcast_fusion.1
  481.0 2.7 copy.45
  483.7 3.6 reshape.153
  (100 shorter events, 15.5 us)
Async XLA Ops:
  0.6 151.3 %collective-permute-start = (s32[512]{0:T(512)}, s32[512]{0:T(512)S(1)}, u32[]{:S(2)}, u32[]{:S(2)}) collective-permute-start(s32[512]{0:T(512)} %param.16), channel_id=1, source_target_pairs={{0,16},{16,0},{1,17},{17,1},{2,18},{18,2},{3,19},{19,3},{4,20},{20... | collective-permute-start | bytes 6152 | tf_op jit(solution)/shard_map/ppermute | solution.py:1086
  7.6 1.1 copy-start.4
  7.7 1.3 copy-start.2
  8.7 1.0 copy-start.5
  8.7 1.0 copy-start.11
  8.7 1.1 copy-start.13
  8.7 1.1 copy-start.14
  8.7 1.1 copy-start.15
  8.7 1.1 copy-start.12
  8.7 1.1 copy-start.16
  8.7 1.1 copy-start.17
  8.8 1.1 copy-start.18
  145.5 6.4 %copy-start.9 = (s32[512]{0:T(512)S(1)}, s32[512]{0:T(512)}, u32[]{:S(2)}) copy-start(s32[512]{0:T(512)} %param.16) | copy-start | bytes 6148
  267.4 2.2 copy-start.1
  269.8 2.8 copy-start.6
  269.8 3.6 copy-start.8
  269.8 3.9 copy-start.7
  271.3 48.7 %collective-permute-start.1 = (bf16[512,2048]{1,0:T(8,128)(2,1)}, bf16[512,2048]{1,0:T(8,128)(2,1)}, u32[]{:S(2)}, u32[]{:S(2)}) collective-permute-start(bf16[512,2048]{1,0:T(8,128)(2,1)} %pad_maximum_fusion.1), channel_id=1, source_target_pairs={{0,16},{16,0},{1,17},{17,1},{2,18},{18,2},{3,19},{19,3},{4,20},{20... | collective-permute-start | bytes 6291464 | tf_op jit(solution)/shard_map/ppermute | solution.py:1102
  320.0 2.5 copy-start.3
  474.9 3.8 copy-start.10
  483.7 3.6 copy-start

commit v2 on v1

--- a/solution.py
+++ b/solution.py
@@ -3,6 +3,7 @@
 
 import jax
 import jax.numpy as jnp
+import numpy as np
 from jax import lax
 from jax.experimental import pallas as pl
 from jax.experimental.pallas import tpu as pltpu
@@ -96,6 +97,27 @@
 
 SWAP = 256
 PARTS = 2
+
+
+def normed_rows(residual):
+    mean_val = jnp.mean(residual, axis=-1, keepdims=True)
+    centred = residual - mean_val
+    variance = jnp.mean(centred * centred, axis=-1, keepdims=True)
+    inv_std = lax.rsqrt(variance + 1e-05)
+    return centred * inv_std, inv_std
+
+
+def norm_back(upstream, normed, inv_std, gain_vec):
+    scaled = upstream * gain_vec
+    return inv_std * (
+        scaled
+        - jnp.mean(scaled, axis=-1, keepdims=True)
+        - normed * jnp.mean(scaled * normed, axis=-1, keepdims=True)
+    )
+
+
+def column_sum(a):
+    return jnp.sum(a, axis=0, keepdims=True)
 
 
 class Gather:
@@ -184,7 +206,7 @@
 
     @property
     def lag(self):
-        return self.hi_count + 2
+        return 2 * self.hi_count + 4
 
     def own_copy(self, sem):
         target = self.full.at[:, self.hi, self.mid, self.core, :, self.mine]
@@ -193,7 +215,8 @@
     def tick(self, t):
         def stage(offset, act):
             if not isinstance(t, int):
-                act(t - offset)
+                chunk = t - offset
+                pl.when((chunk >= 0) & (chunk < self.count))(lambda: act(chunk))
             elif 0 <= t - offset < self.count:
                 act(t - offset)
 
@@ -228,10 +251,10 @@
 
         stage(0, own)
         for distance in range(1, self.hi_count):
-            stage(distance, functools.partial(forward, distance))
-        stage(self.hi_count, after_y)
-        stage(self.hi_count + 1, after_x)
-        stage(self.hi_count + 2, after_c)
+            stage(2 * distance, functools.partial(forward, distance))
+        stage(2 * self.hi_count, after_y)
+        stage(2 * self.hi_count + 2, after_x)
+        stage(2 * self.hi_count + 4, after_c)
 
     def drain(self):
         @pl.loop(0, self.count)
@@ -264,55 +287,371 @@
     pl.semaphore_wait(barrier, 5 - first.astype(jnp.int32) - last.astype(jnp.int32))
 
 
-def gather_kernel(hi_count, packed, vec, tokens, full, vec_full, tokens_all, local_sem, t_sem, *sems):
+UP, DOWN = 4, 5
+HALF = D // 2
+QUAD = 4 * HEAD_DIM
+B_OUT, GAIN_ONE, SHIFT_ONE, B_UP, B_DOWN, GAIN_TWO, SHIFT_TWO = 3, 4, 5, 6, 10, 11, 12
+VEC_ROWS = 16
+
+
+def regroup(pieces, depth):
+    out = None
+    for u, (tile, start) in enumerate(pieces):
+        shift = (u * depth - start) % LANES
+        moved = pltpu.roll(tile, shift, 1) if shift else tile
+        lane = lax.broadcasted_iota(jnp.int32, moved.shape, 1)
+        out = moved if out is None else jnp.where(lane // depth == u, moved, out)
+    return out
+
+
+def tile_of(at):
+    return slice(at // LANES * LANES, at // LANES * LANES + LANES)
+
+
+def pack(packed, w_qkv, w_out, w_up, w_down):
+    depth = w_qkv.shape[0]
+    for slab in range(3):
+        packed[slab] = w_qkv[:, slab * D : (slab + 1) * D].astype(BF)
+    packed[3] = w_out[...].astype(BF)
+    each = LANES // depth
+    for j in range(4):
+        packed[DOWN + 2 * j] = w_down[j * depth : (j + 1) * depth].astype(BF)
+        for t in range(D // LANES):
+            starts = [4 * depth * (t * each + u) + depth * j for u in range(each)]
+            pieces = [(w_up[:, tile_of(at)], at % LANES) for at in starts]
+            packed[UP + 2 * j, :, t * LANES : (t + 1) * LANES] = regroup(pieces, depth).astype(BF)
+
+
+def unpack_vectors(vec_full, rows_out, bias, depth):
+    hi_count = vec_full.shape[1]
+    each = LANES // depth
+
+    def of_shard(shard):
+        return vec_full[0, shard // 4, shard // 2 % 2, shard % 2].astype(F32)
+
+    def join(pieces):
+        lane = lax.broadcasted_iota(jnp.int32, pieces[0].shape, 1)
+        out = pieces[0]
+        for u in range(1, each):
+            out = jnp.where(lane // depth == u, pieces[u], out)
+        return out
+
+    for t in range(D // LANES):
+        tile = slice(t * LANES, (t + 1) * LANES)
+        rows_out[:, tile] = join([of_shard(t * each + u) for u in range(each)])
+        for j in range(3):
+            chunks = [(j * D + t * LANES) // depth + u for u in range(each)]
+            bias[j : j + 1, tile] = join([of_shard(m // 3)[m % 3 : m % 3 + 1] for m in chunks])
+
+
+def gelu_parts(hidden):
+    gauss = jnp.exp(hidden * hidden * -0.5)
+    t = 1.0 / (1.0 + (ERFC_P * math.sqrt(0.5)) * jnp.abs(hidden))
+    poly = jnp.full_like(t, ERFC_Q[-1])
+    for coefficient in ERFC_Q[-2::-1]:
+        poly = poly * t + coefficient
+    tail = 0.5 * t * poly * gauss
+    cdf = jnp.where(hidden >= 0, 1.0 - tail, tail)
+    return hidden * cdf, cdf + hidden * gauss * (1.0 / math.sqrt(2.0 * math.pi))
+
+
+def forward_kernel(
+    hi_count,
+    w_qkv,
+    w_out,
+    w_up,
+    w_down,
+    vec,
+    tokens,
+    cotangent,
+    q_doc,
+    cosine,
+    sine,
+    full,
+    q_all,
+    k_all,
+    v_all,
+    q_ext_all,
+    active_all,
+    slope_all,
+    k_doc,
+    context,
+    first_low,
+    normed_out,
+    inv_out,
+    result,
+    d_second,
+    d_ffn,
+    sums,
+    vectors,
+    packed,
+    vec_full,
+    x_peer,
+    slots,
+    q_buf,
+    k_buf,
+    v_buf,
+    ext_buf,
+    first,
+    total,
+    act_buf,
+    slope_buf,
+    bias,
+    local_sem,
+    load_sem,
+    flush_sem,
+    t_sem,
+    *sems,
+):
+    rows = tokens.shape[0]
+    depth = w_qkv.shape[0]
     rep = lax.axis_index("rep")
     gather = Gather(hi_count, packed, full, sems[:10])
     small = Gather(hi_count, vec, vec_full, sems[10:], swap=0)
+    lane_doc = lax.broadcasted_iota(jnp.int32, (rows, LANES), 1)
+    other = jnp.where(q_doc[...] > 0.5, 0.0, MASKED)
+    other = jnp.where(lane_doc < 61, other, jnp.where(lane_doc < 64, 1.0, 0.0))
+    k_doc[:rows] = other.astype(BF)
+    pack(packed, w_qkv, w_out, w_up, w_down)
     near_barrier(hi_count)
-    token_copy = remote(tokens, tokens_all.at[1], t_sem.at[0], t_sem.at[1], {"rep": 1 - rep})
-    token_copy.start()
-    copies = [
-        pltpu.make_async_copy(tokens, tokens_all.at[0], local_sem.at[0]),
-        small.own_copy(local_sem.at[1]),
-        gather.own_copy(local_sem.at[2]),
-    ]
+    peer = {"rep": 1 - rep}
+    token_copy = remote(tokens, x_peer, t_sem.at[0], t_sem.at[1], peer)
+    doc_copy = remote(k_doc.at[:rows], k_doc.at[rows:], t_sem.at[2], t_sem.at[3], peer)
+    copies = [small.own_copy(local_sem.at[0]), gather.own_copy(local_sem.at[1])]
     for copy in copies:
         copy.start()
+    doc_copy.start()
+    token_copy.start()
     for copy in copies:
         copy.wait()
-    for t in range(gather.lag + 1):
+    warm = gather.lag + 1
+    for t in range(warm):
         small.tick(t)
         gather.tick(t)
-
-    @pl.loop(gather.lag + 1, gather.count)
+    unpack_vectors(vec_full, vectors, bias, depth)
+    doc_copy.wait()
+    token_copy.wait()
+    ready = 3 * gather.parts + gather.lag
+
+    @pl.loop(warm, ready)
     def _(t):
         gather.tick(t)
 
-    for t in range(gather.count, gather.count + gather.lag):
-        gather.tick(t)
-    token_copy.wait()
+    def load_whole(slab, slot):
+        return pltpu.make_async_copy(full.at[slab], slots.at[slot], load_sem.at[slot])
+
+    for slab in range(3):
+        load_whole(slab, slab).start()
+    for slab in range(3):
+        load_whole(slab, slab).wait()
+
+    def weight(slot, columns):
+        return slots[slot, :, :, :, :, columns].reshape(D, -1)
+
+    own_rows = pl.ds(pl.multiple_of(rep * rows, rows), rows)
+    peer_rows = pl.ds(pl.multiple_of((1 - rep) * rows, rows), rows)
+
+    def rope(a, table_rows):
+        cos_part, sin_part = cosine[table_rows, :], sine[table_rows, :]
+        cos_part = jnp.concatenate([cos_part, cos_part], axis=1)
+        sin_part = jnp.concatenate([sin_part, sin_part], axis=1)
+        return a * cos_part + swap_halves(a) * sin_part
+
+    def flushes(i):
+        return [
+            pltpu.make_async_copy(q_buf.at[i], q_all.at[i], flush_sem.at[0, i]),
+            pltpu.make_async_copy(k_buf.at[i], k_all.at[i], flush_sem.at[1, i]),
+            pltpu.make_async_copy(v_buf.at[i], v_all.at[i], flush_sem.at[2, i]),
+            pltpu.make_async_copy(
+                ext_buf.at[pl.ds(4 * i, 4)], q_ext_all.at[pl.ds(4 * i, 4)], flush_sem.at[3, i]
+            ),
+        ]
+
+    ones = jnp.ones((2 * rows, LANES), BF)
+    piece = 256
+
+    @pl.loop(0, HEADS // 4)
+    def _(i):
+        columns = pl.ds(pl.multiple_of(i * QUAD, QUAD), QUAD)
+        own_x, peer_x = tokens[...], x_peer[...]
+        w = weight(0, columns)
+        q_rows = rope(dot(own_x, w) + bias[0:1, columns], own_rows) * HEAD_DIM**-0.5
+        q_buf[i] = q_rows.astype(BF)
+        w = weight(1, columns)
+        k_buf[i, :rows] = rope(dot(own_x, w) + bias[1:2, columns], own_rows).astype(BF)
+        k_buf[i, rows:] = rope(dot(peer_x, w) + bias[1:2, columns], peer_rows).astype(BF)
+        w = weight(2, columns)
+        v_buf[i, :rows] = (dot(own_x, w) + bias[2:3, columns]).astype(BF)
+        v_buf[i, rows:] = (dot(peer_x, w) + bias[2:3, columns]).astype(BF)
+        for pair in range(2):
+            gather.tick(ready + 2 * i + pair)
+            lanes = slice(pair * LANES, (pair + 1) * LANES)
+            keys = jnp.concatenate([k_buf[i, :, lanes], k_doc[...]], axis=1)
+            values = jnp.concatenate([v_buf[i, :, lanes], ones], axis=1)
+            for start in range(0, rows, piece):
+                part = slice(start, start + piece)
+                q_pair = q_buf[i, part, lanes]
+                lane = lax.broadcasted_iota(jnp.int32, q_pair.shape, 1)
+                doc_q = q_doc[part, :]
+                mixed = []
+                for head in range(2):
+                    in_head = (lane // HEAD_DIM) == head
+                    queries = jnp.concatenate([jnp.where(in_head, q_pair, 0), doc_q], axis=1)
+                    scores = dot_nt(queries, keys)
+                    row_max = jnp.max(scores, axis=1, keepdims=True)
+                    prob = jnp.exp(scores - row_max).astype(BF)
+                    both = dot(prob, values)
+                    row_sum = both[:, LANES:]
+                    mixed.append(both[:, :LANES] / row_sum)
+                    hi, mid, low = split3(-(row_max + jnp.log(row_sum)))
+                    ext = jnp.where(lane == 61, hi, doc_q)
+                    ext = jnp.where(lane == 62, mid, ext)
+                    ext = jnp.where(lane == 63, low, ext)
+                    ext_buf[4 * i + pair * 2 + head, part, :] = ext
+                pair_lanes = pl.ds(pl.multiple_of(i * QUAD + pair * LANES, LANES), LANES)
+                context[part, pair_lanes] = jnp.where(lane < HEAD_DIM, mixed[0], mixed[1]).astype(BF)
+        for copy in flushes(i):
+            copy.start()
+
+    done = ready + HEADS // 2
+
+    def vector(row):
+        return vectors[row : row + 1, :]
+
+    load_whole(3, 3).start()
+    for slot in range(2):
+        load_whole(UP + slot, slot).start()
+    load_whole(3, 3).wait()
+    attn = dot(context[...], weight(3, slice(None))) + vector(B_OUT)
+    normed, inv_std = normed_rows(tokens[...].astype(F32) + attn)
+    first[...] = normed * vector(GAIN_ONE) + vector(SHIFT_ONE)
+    first_low[...] = first[...].astype(BF)
+    normed_out[...] = normed
+    inv_out[...] = jnp.broadcast_to(inv_std, inv_out.shape)
+    total[...] = first[...] + vector(B_DOWN)
+
+    def keeps(j, half):
+        return [
+            pltpu.make_async_copy(
+                act_buf.at[half], active_all.at[2 * j + half], flush_sem.at[4, 2 * half]
+            ),
+            pltpu.make_async_copy(
+                slope_buf.at[half], slope_all.at[2 * j + half], flush_sem.at[4, 2 * half + 1]
+            ),
+        ]
+
+    @pl.loop(0, 4)
+    def _(j):
+        base = lax.rem(j, 2) * 2
+
+        for slot in range(2):
+            load_whole(UP + 2 * j + slot, base + slot).wait()
+        for half in range(2):
+            @pl.when(j > 0)
+            def _():
+                for copy in keeps(j - 1, half):
+                    copy.wait()
+
+            columns = slice(half * HALF, (half + 1) * HALF)
+            hidden = dot(first_low[...], weight(base, columns)) + vectors[pl.ds(B_UP + j, 1), columns]
+            act, slope = gelu_parts(hidden)
+            act_buf[half] = act.astype(BF)
+            slope_buf[half] = slope.astype(BF)
+            down = slots[base + 1, half * (hi_count // 2) : (half + 1) * (hi_count // 2)].reshape(HALF, D)
+            total[...] += dot(act_buf[half], down)
+            for copy in keeps(j, half):
+                copy.start()
+            for step in range(2):
+                t = 6 * gather.parts + gather.lag + 2 * gather.parts * j + gather.parts * half + step
+                if step < gather.parts:
+                    pl.when(t >= done)(lambda: gather.tick(t))
+
+        @pl.when(j < 3)
+        def _():
+            for slot in range(2):
+                load_whole(UP + 2 * j + 2 + slot, 2 - base + slot).start()
+
+    for half in range(2):
+        for copy in keeps(3, half):
+            copy.wait()
+    gain = vector(GAIN_TWO)
+    normed, inv_std = normed_rows(total[...])
+    result[...] = (normed * gain + vector(SHIFT_TWO)).astype(BF)
+    up = cotangent[...].astype(F32)
+    sums[0:1] = column_sum(up * normed)
+    sums[1:2] = column_sum(up)
+    grad = norm_back(up, normed, inv_std, gain)
+    d_second[...] = grad
+    low = grad.astype(BF)
+    d_ffn[...] = low
+    sums[2:3] = column_sum(low.astype(F32))
     small.drain()
     gather.drain()
 
-
-def gather(hi_count, packed, vec, tokens):
-    rows = packed.shape[1]
+    @pl.loop(0, HEADS // 4)
+    def _(i):
+        for copy in flushes(i):
+            copy.wait()
+
+
+def forward(hi_count, weights, vec, tokens, cotangent, q_doc, cosine, sine):
+    rows = tokens.shape[0]
+    depth = weights[0].shape[0]
     anywhere = pl.BlockSpec(memory_space=pl.ANY)
+    vmem = pl.BlockSpec(memory_space=pltpu.VMEM)
+    dma = pltpu.SemaphoreType.DMA
+    quads = HEADS // 4
+    shape = jax.ShapeDtypeStruct
+    blocks = (hi_count, 2, 2, depth, D)
     return pl.pallas_call(
-        functools.partial(gather_kernel, hi_count),
+        functools.partial(forward_kernel, hi_count),
         out_shape=(
-            jax.ShapeDtypeStruct((SLABS, hi_count, 2, 2, rows, D), BF),
-            jax.ShapeDtypeStruct((1, hi_count, 2, 2) + vec.shape, BF),
-            jax.ShapeDtypeStruct((2,) + tokens.shape, BF),
+            shape((SLABS,) + blocks, BF),
+            shape((quads, rows, QUAD), BF),
+            shape((quads, 2 * rows, QUAD), BF),
+            shape((quads, 2 * rows, QUAD), BF),
+            shape((HEADS, rows, LANES), BF),
+            shape((8, rows, HALF), BF),
+            shape((8, rows, HALF), BF),
+            shape((2 * rows, LANES), BF),
+            shape((rows, D), BF),
+            shape((rows, D), BF),
+            shape((rows, D), F32),
+            shape((rows, LANES), F32),
+            shape((rows, D), BF),
+            shape((rows, D), F32),
+            shape((rows, D), BF),
+            shape((3, D), F32),
+            shape((VEC_ROWS, D), F32),
         ),
-        in_specs=[pl.BlockSpec(memory_space=pltpu.VMEM)] * 3,
-        out_specs=(anywhere,) * 3,
-        scratch_shapes=[pltpu.SemaphoreType.DMA((3,)), pltpu.SemaphoreType.DMA((2,))]
-        + Gather.scratch(hi_count, SLABS, rows)
-        + Gather.scratch(hi_count, 1, vec.shape[0], swap=0),
-        compiler_params=pltpu.CompilerParams(collective_id=0, has_side_effects=True),
-        name="gather",
-    )(packed, vec[None], tokens)
+        in_specs=[vmem] * 10,
+        out_specs=(anywhere,) * 7 + (vmem,) * 10,
+        scratch_shapes=[
+            pltpu.VMEM((SLABS, depth, D), BF),
+            pltpu.VMEM((1, hi_count, 2, 2) + vec.shape[1:], BF),
+            pltpu.VMEM((rows, D), BF),
+            pltpu.VMEM((4,) + blocks, BF),
+            pltpu.VMEM((quads, rows, QUAD), BF),
+            pltpu.VMEM((quads, 2 * rows, QUAD), BF),
+            pltpu.VMEM((quads, 2 * rows, QUAD), BF),
+            pltpu.VMEM((HEADS, rows, LANES), BF),
+            pltpu.VMEM((rows, D), F32),
+            pltpu.VMEM((rows, D), F32),
+            pltpu.VMEM((2, rows, HALF), BF),
+            pltpu.VMEM((2, rows, HALF), BF),
+            pltpu.VMEM((3, D), F32),
+            dma((2,)),
+            dma((4,)),
+            dma((5, quads)),
+            dma((4,)),
+        ]
+        + Gather.scratch(hi_count, SLABS, depth)
+        + Gather.scratch(hi_count, 1, vec.shape[1], swap=0),
+        compiler_params=pltpu.CompilerParams(
+            collective_id=0, has_side_effects=True, vmem_limit_bytes=VMEM
+        ),
+        name="forward",
+    )(*weights, vec, tokens, cotangent, q_doc, cosine, sine)
 
 
 def scatter_kernel(
@@ -585,102 +924,15 @@
     )
 
 
-QUAD = 4 * HEAD_DIM
-
-
-def attend_kernel(
-    tokens, w_q, w_k, w_v, bias, cosine, sine, q_doc, k_doc, q_out, k_out, v_out, context, q_ext
-):
-    own_rows = q_out.shape[0]
-    x = tokens[...]
-    cos_all = jnp.concatenate([cosine[...], cosine[...]], axis=1)
-    sin_all = jnp.concatenate([sine[...], sine[...]], axis=1)
-
-    def rope(a, count):
-        return a * cos_all[:count] + swap_halves(a) * sin_all[:count]
-
-    q_rows = rope(dot(x[:own_rows], w_q[0]) + bias[0:1], own_rows) * HEAD_DIM**-0.5
-    q_out[...] = q_rows.astype(BF)
-    k_out[...] = rope(dot(x, w_k[0]) + bias[1:2], 2 * own_rows).astype(BF)
-    v_out[...] = (dot(x, w_v[0]) + bias[2:3]).astype(BF)
-    doc_k = k_doc[...]
-    ones = jnp.ones((2 * own_rows, LANES), BF)
-    piece = 256
-    for pair in range(2):
-        lanes = slice(pair * LANES, (pair + 1) * LANES)
-        keys = jnp.concatenate([k_out[:, lanes], doc_k], axis=1)
-        values = jnp.concatenate([v_out[:, lanes], ones], axis=1)
-        for start in range(0, own_rows, piece):
-            rows = slice(start, start + piece)
-            q_pair = q_out[rows, lanes]
-            lane = lax.broadcasted_iota(jnp.int32, q_pair.shape, 1)
-            doc_q = q_doc[rows, :]
-            mixed = []
-            for head in range(2):
-                in_head = (lane // HEAD_DIM) == head
-                queries = jnp.concatenate([jnp.where(in_head, q_pair, 0), doc_q], axis=1)
-                scores = dot_nt(queries, keys)
-                row_max = jnp.max(scores, axis=1, keepdims=True)
-                prob = jnp.exp(scores - row_max).astype(BF)
-                both = dot(prob, values)
-                row_sum = both[:, LANES:]
-                mixed.append(both[:, :LANES] / row_sum)
-                log_total = row_max + jnp.log(row_sum)
-                hi, mid, low = split3(-log_total)
-                ext = jnp.where(lane == 61, hi, doc_q)
-                ext = jnp.where(lane == 62, mid, ext)
-                ext = jnp.where(lane == 63, low, ext)
-                q_ext[pair * 2 + head, rows, :] = ext
-            context[rows, lanes] = jnp.where(lane < HEAD_DIM, mixed[0], mixed[1]).astype(BF)
-
-
-def attend(tokens_all, full, bias, cosine, sine, q_doc, k_doc):
-    rows = tokens_all.shape[0] // 2
-    whole = lambda *shape: pl.BlockSpec(shape, lambda i: (0,) * len(shape))
-    weight = lambda slab: pl.BlockSpec((1, D, QUAD), lambda i: (slab, 0, i))
-    columns = lambda count: pl.BlockSpec((count, QUAD), lambda i: (0, i))
-    return pl.pallas_call(
-        attend_kernel,
-        grid=(HEADS // 4,),
-        out_shape=(
-            jax.ShapeDtypeStruct((rows, D), BF),
-            jax.ShapeDtypeStruct((2 * rows, D), BF),
-            jax.ShapeDtypeStruct((2 * rows, D), BF),
-            jax.ShapeDtypeStruct((rows, D), BF),
-            jax.ShapeDtypeStruct((HEADS, rows, LANES), BF),
-        ),
-        in_specs=[
-            whole(2 * rows, D),
-            weight(0),
-            weight(1),
-            weight(2),
-            columns(3),
-            whole(2 * rows, LANES),
-            whole(2 * rows, LANES),
-            whole(rows, LANES),
-            whole(2 * rows, LANES),
-        ],
-        out_specs=(
-            columns(rows),
-            columns(2 * rows),
-            columns(2 * rows),
-            columns(rows),
-            pl.BlockSpec((4, rows, LANES), lambda i: (i, 0, 0)),
-        ),
-        compiler_params=pltpu.CompilerParams(vmem_limit_bytes=VMEM),
-        name="attend",
-    )(tokens_all, full, full, full, bias, cosine, sine, q_doc, k_doc)
-
-
 def attend_back_kernel(
     q_in, k_in, v_in, context, d_context, q_ext, k_doc, cosine, sine, d_q, d_k, d_v
 ):
-    own_rows = q_in.shape[0]
+    own_rows = q_in.shape[1]
     doc_k = k_doc[...]
     for pair in range(2):
         lanes = slice(pair * LANES, (pair + 1) * LANES)
-        k_pair, v_pair = k_in[:, lanes], v_in[:, lanes]
-        q_pair, g_pair = q_in[:, lanes], d_context[:, lanes]
+        k_pair, v_pair = k_in[0, :, lanes], v_in[0, :, lanes]
+        q_pair, g_pair = q_in[0, :, lanes], d_context[:, lanes]
         lane = lax.broadcasted_iota(jnp.int32, q_pair.shape, 1)
         k_lane = lax.broadcasted_iota(jnp.int32, k_pair.shape, 1)
         keys = jnp.concatenate([k_pair, doc_k], axis=1)
@@ -714,7 +966,7 @@
 
 
 def attend_back(q, k, v, context, d_context, q_ext, k_doc, cosine, sine):
-    rows = q.shape[0]
+    rows = q.shape[1]
     whole = lambda *shape: pl.BlockSpec(shape, lambda i: (0,) * len(shape))
     columns = lambda count: pl.BlockSpec((count, QUAD), lambda i: (0, i))
     return pl.pallas_call(
@@ -726,9 +978,9 @@
             jax.ShapeDtypeStruct((2 * rows, D), BF),
         ),
         in_specs=[
-            columns(rows),
-            columns(2 * rows),
-            columns(2 * rows),
+            pl.BlockSpec((1, rows, QUAD), lambda i: (i, 0, 0)),
+            pl.BlockSpec((1, 2 * rows, QUAD), lambda i: (i, 0, 0)),
+            pl.BlockSpec((1, 2 * rows, QUAD), lambda i: (i, 0, 0)),
             columns(rows),
             columns(rows),
             pl.BlockSpec((4, rows, LANES), lambda i: (i, 0, 0)),
@@ -742,143 +994,8 @@
     )(q, k, v, context, d_context, q_ext, k_doc, cosine, sine)
 
 
-def normed_rows(residual):
-    mean_val = jnp.mean(residual, axis=-1, keepdims=True)
-    centred = residual - mean_val
-    variance = jnp.mean(centred * centred, axis=-1, keepdims=True)
-    inv_std = lax.rsqrt(variance + 1e-05)
-    return centred * inv_std, inv_std
-
-
-def norm_back(upstream, normed, inv_std, gain_vec):
-    scaled = upstream * gain_vec
-    return inv_std * (
-        scaled
-        - jnp.mean(scaled, axis=-1, keepdims=True)
-        - normed * jnp.mean(scaled * normed, axis=-1, keepdims=True)
-    )
-
-
-def column_sum(a):
-    return jnp.sum(a, axis=0, keepdims=True)
-
-
 CHUNK = 512
 CHUNKS = FF // CHUNK
-
-
-def forward_kernel(
-    tokens,
-    context,
-    w_out,
-    cotangent,
-    vectors,
-    b_up,
-    w_up,
-    w_down,
-    result,
-    first_out,
-    normed_out,
-    inv_out,
-    active,
-    slope,
-    d_second,
-    d_ffn,
-    sums,
-    first,
-    total,
-):
-    step = pl.program_id(0)
-
-    @pl.when(step == 0)
-    def _():
-        attn = dot(context[...], w_out[0]) + vectors[0:1]
-        normed, inv_std = normed_rows(tokens[0].astype(F32) + attn)
-        first[...] = normed * vectors[1:2] + vectors[2:3]
-        first_out[...] = first[...].astype(BF)
-        normed_out[...] = normed
-        inv_out[...] = jnp.broadcast_to(inv_std, inv_out.shape)
-
-    hidden = dot(first_out[...], w_up[0]) + b_up[...]
-    gauss = jnp.exp(hidden * hidden * -0.5)
-    t = 1.0 / (1.0 + (ERFC_P * math.sqrt(0.5)) * jnp.abs(hidden))
-    poly = jnp.full_like(t, ERFC_Q[-1])
-    for coefficient in ERFC_Q[-2::-1]:
-        poly = poly * t + coefficient
-    tail = 0.5 * t * poly * gauss
-    cdf = jnp.where(hidden >= 0, 1.0 - tail, tail)
-    act = (hidden * cdf).astype(BF)
-    active[...] = act
-    slope[...] = (cdf + hidden * gauss * (1.0 / math.sqrt(2.0 * math.pi))).astype(slope.dtype)
-    part = dot(act, w_down[0])
-
-    @pl.when(step == 0)
-    def _():
-        total[...] = part
-
-    @pl.when(step > 0)
-    def _():
-        total[...] += part
-
-    @pl.when(step == CHUNKS - 1)
-    def _():
-        gain = vectors[4:5]
-        normed, inv_std = normed_rows(first[...] + total[...] + vectors[3:4])
-        result[...] = (normed * gain + vectors[5:6]).astype(BF)
-        up = cotangent[...].astype(F32)
-        sums[0:1] = column_sum(up * normed)
-        sums[1:2] = column_sum(up)
-        grad = norm_back(up, normed, inv_std, gain)
-        d_second[...] = grad
-        low = grad.astype(BF)
-        d_ffn[...] = low
-        sums[2:3] = column_sum(low.astype(F32))
-
-
-def forward(tokens_all, context, full, cotangent, vectors, b_up):
-    rows = context.shape[0]
-    per = D // CHUNK
-    whole = lambda *shape: pl.BlockSpec(shape, lambda i: (0,) * len(shape))
-    wide = pl.BlockSpec((rows, CHUNK), lambda i: (0, i))
-    return pl.pallas_call(
-        forward_kernel,
-        grid=(CHUNKS,),
-        out_shape=(
-            jax.ShapeDtypeStruct((rows, D), BF),
-            jax.ShapeDtypeStruct((rows, D), BF),
-            jax.ShapeDtypeStruct((rows, D), F32),
-            jax.ShapeDtypeStruct((rows, LANES), F32),
-            jax.ShapeDtypeStruct((rows, FF), BF),
-            jax.ShapeDtypeStruct((rows, FF), F32),
-            jax.ShapeDtypeStruct((rows, D), F32),
-            jax.ShapeDtypeStruct((rows, D), BF),
-            jax.ShapeDtypeStruct((3, D), F32),
-        ),
-        in_specs=[
-            pl.BlockSpec((1, rows, D), lambda i: (0, 0, 0)),
-            whole(rows, D),
-            pl.BlockSpec((1, D, D), lambda i: (3, 0, 0)),
-            whole(rows, D),
-            whole(6, D),
-            pl.BlockSpec((1, CHUNK), lambda i: (0, i)),
-            pl.BlockSpec((1, D, CHUNK), lambda i: (4 + i // per, 0, i % per)),
-            pl.BlockSpec((1, CHUNK, D), lambda i: (8 + i // per, i % per, 0)),
-        ],
-        out_specs=(
-            whole(rows, D),
-            whole(rows, D),
-            whole(rows, D),
-            whole(rows, LANES),
-            wide,
-            wide,
-            whole(rows, D),
-            whole(rows, D),
-            whole(3, D),
-        ),
-        scratch_shapes=[pltpu.VMEM((rows, D), F32), pltpu.VMEM((rows, D), F32)],
-        compiler_params=pltpu.CompilerParams(vmem_limit_bytes=VMEM),
-        name="forward",
-    )(tokens_all, context, full, cotangent, vectors, b_up, full, full)
 
 
 def backward_kernel(
@@ -905,8 +1022,8 @@
 ):
     step = pl.program_id(0)
     low = d_ffn[...]
-    d_hidden = (dot_nt(low, w_down[0]) * slope[...]).astype(BF)
-    g_down[...] = dot_tn(active[...], low).astype(BF)
+    d_hidden = (dot_nt(low, w_down[0]) * slope[0].astype(F32)).astype(BF)
+    g_down[...] = dot_tn(active[0], low).astype(BF)
     g_up[...] = dot_tn(first[...], d_hidden).astype(BF)
     g_b_up[...] = column_sum(d_hidden.astype(F32))
     part = dot_nt(d_hidden, w_up[0])
@@ -924,7 +1041,7 @@
         up = total[...]
         sums[0:1] = column_sum(up * normed[...])
         sums[1:2] = column_sum(up)
-        grad = norm_back(up, normed[...], inv_std[:, 0:1], vectors[1:2])
+        grad = norm_back(up, normed[...], inv_std[:, 0:1], vectors[GAIN_ONE : GAIN_ONE + 1])
         d_resid[...] = grad
         d_attn = grad.astype(BF)
         sums[2:3] = column_sum(d_attn.astype(F32))
@@ -936,7 +1053,7 @@
     rows = context.shape[0]
     per = D // CHUNK
     whole = lambda *shape: pl.BlockSpec(shape, lambda i: (0,) * len(shape))
-    wide = pl.BlockSpec((rows, CHUNK), lambda i: (0, i))
+    wide = pl.BlockSpec((1, rows, HALF), lambda i: (i, 0, 0))
     return pl.pallas_call(
         backward_kernel,
         grid=(CHUNKS,),
@@ -956,12 +1073,12 @@
             whole(rows, D),
             whole(rows, LANES),
             whole(rows, D),
-            whole(6, D),
+            whole(VEC_ROWS, D),
             pl.BlockSpec((1, D, D), lambda i: (3, 0, 0)),
             wide,
             wide,
-            pl.BlockSpec((1, D, CHUNK), lambda i: (4 + i // per, 0, i % per)),
-            pl.BlockSpec((1, CHUNK, D), lambda i: (8 + i // per, i % per, 0)),
+            pl.BlockSpec((1, D, CHUNK), lambda i: (UP + 2 * (i // per), 0, i % per)),
+            pl.BlockSpec((1, CHUNK, D), lambda i: (DOWN + 2 * (i // per), i % per, 0)),
         ],
         out_specs=(
             pl.BlockSpec((CHUNK, D), lambda i: (i, 0)),
@@ -981,7 +1098,7 @@
 def project_back_kernel(tokens, d_joined, d_resid, weight, g_qkv, g_bias, input_grad):
     step = pl.program_id(0)
     low = d_joined[...]
-    g_qkv[...] = dot_tn(tokens[0], low).astype(BF)
+    g_qkv[...] = dot_tn(tokens[...], low).astype(BF)
     g_bias[...] = column_sum(low.astype(F32))
     part = dot_nt(low, weight[0])
 
@@ -1007,7 +1124,7 @@
             jax.ShapeDtypeStruct((rows, D), F32),
         ),
         in_specs=[
-            pl.BlockSpec((1, rows, D), lambda i: (0, 0, 0)),
+            whole(rows, D),
             pl.BlockSpec((rows, CHUNK), lambda i: (0, i)),
             whole(rows, D),
             pl.BlockSpec((1, D, CHUNK), lambda i: (i // per, 0, i % per)),
@@ -1022,18 +1139,14 @@
     )(tokens_all, d_joined, d_resid, full)
 
 
-def rope_tables(rows):
-    half = lax.axis_index("rep")
-    index = jnp.arange(2 * rows, dtype=jnp.int32)
-    position = ((index + half * rows) % (2 * rows)).astype(F32)
-    frequency = jnp.exp(
-        jnp.arange(HEAD_DIM // 2, dtype=F32) * (-2.0 * math.log(10000.0) / HEAD_DIM)
-    )
-    angles = position[:, None] * frequency[None, :]
-    cosine, sine = jnp.cos(angles), jnp.sin(angles)
+def rope_tables(count):
+    position = np.arange(count, dtype=np.float32)
+    frequency = np.exp(np.arange(HEAD_DIM // 2, dtype=np.float32) * np.float32(-2.0 * math.log(10000.0) / HEAD_DIM))
+    angles = position[:, None] * frequency[None, :].astype(np.float32)
+    cosine, sine = np.cos(angles).astype(np.float32), np.sin(angles).astype(np.float32)
     return (
-        jnp.concatenate([cosine] * 4, axis=1),
-        jnp.concatenate([-sine, sine, -sine, sine], axis=1),
+        jnp.asarray(np.concatenate([cosine] * 4, axis=1)),
+        jnp.asarray(np.concatenate([-sine, sine, -sine, sine], axis=1)),
     )
 
 
@@ -1058,53 +1171,30 @@
     shards = lax.axis_size("shard")
     hi_count = shards // 4
     depth = D // shards
-    packed = jnp.concatenate(
-        [
-            w_qkv.astype(BF).reshape(depth, 3, D).transpose(1, 0, 2),
-            w_out.astype(BF)[None],
-            w_up.astype(BF).reshape(depth, shards, 4, depth).transpose(2, 0, 1, 3).reshape(4, depth, D),
-            w_down.astype(BF).reshape(4, depth, D),
-        ],
-        axis=0,
-    )
     small = (b_qkv, b_out, gain_one, shift_one, b_up, b_down, gain_two, shift_two)
     widths = [a.shape[0] for a in small]
-    flat = jnp.concatenate([a.astype(BF) for a in small])
-    flat = jnp.pad(flat, (0, -flat.shape[0] % (16 * LANES)))
-    full, vec_full, tokens_all = gather(hi_count, packed, flat.reshape(-1, LANES), tokens)
-    full = full.reshape(SLABS, D, D)
-    vec_rows = vec_full.reshape(shards, flat.shape[0]).astype(F32)
-    parts = []
-    at = 0
-    for width in widths:
-        parts.append(vec_rows[:, at : at + width])
-        at += width
-    bias_qkv = parts[0].reshape(3, D)
-    bias_up = parts[4].reshape(shards, 4, depth).transpose(1, 0, 2).reshape(1, FF)
-    vectors = jnp.stack([parts[i].reshape(D) for i in (1, 2, 3, 5, 6, 7)])
-
-    seg_peer = lax.ppermute(segments, "rep", [(0, 1), (1, 0)])
-    seg_all = jnp.concatenate([segments, seg_peer])
+    vec = jnp.concatenate(small).astype(BF).reshape(-1, depth)
+    vec = jnp.tile(jnp.pad(vec, ((0, VEC_ROWS - vec.shape[0]), (0, 0))), (1, LANES // depth))
     lane = jnp.arange(LANES, dtype=jnp.int32)[None, :]
     q_doc = (segments[:, None] == lane).astype(BF)
-    k_doc = jnp.where((seg_all[:, None] == lane) | (lane >= 64), 0.0, MASKED)
-    k_doc = jnp.where((lane >= 61) & (lane < 64), 1.0, k_doc).astype(BF)
-    cosine, sine = rope_tables(rows)
-    both = tokens_all.reshape(2 * rows, D)
-    q, k, v, context, q_ext = attend(both, full, bias_qkv, cosine, sine, q_doc, k_doc)
-    result, first, normed, inv_std, active, slope, d_second, d_ffn, sums_two = forward(
-        tokens_all, context, full, cotangent, vectors, bias_up
-    )
+    cosine, sine = rope_tables(2 * rows)
+    (
+        full, q, k, v, q_ext, active, slope, k_doc, context, first, normed, inv_std, result,
+        d_second, d_ffn, sums_two, vectors,
+    ) = forward(hi_count, (w_qkv, w_out, w_up, w_down), vec[None], tokens, cotangent, q_doc, cosine, sine)
+    full = full.reshape(SLABS, D, D)
     g_down, g_up, g_b_up, g_out, d_resid, d_context, sums_one = backward(
         d_ffn, d_second, first, normed, inv_std, context, vectors, full, active, slope
     )
+    half = lax.axis_index("rep")
+    cosine, sine = jnp.roll(cosine, half * rows, axis=0), jnp.roll(sine, half * rows, axis=0)
     d_q, d_k, d_v = attend_back(q, k, v, context, d_context, q_ext, k_doc, cosine, sine)
     peer = lax.ppermute(
         jnp.concatenate([d_k[rows:], d_v[rows:]], axis=1), "rep", [(0, 1), (1, 0)]
     ).astype(F32)
     own = jnp.concatenate([d_k[:rows], d_v[:rows]], axis=1).astype(F32)
     d_joined = jnp.concatenate([d_q, (own + peer).astype(BF)], axis=1)
-    g_qkv, g_b_qkv, input_grad = project_back(tokens_all, d_joined, d_resid, full)
+    g_qkv, g_b_qkv, input_grad = project_back(tokens, d_joined, d_resid, full)
 
     g_b_up = g_b_up.reshape(4, shards, depth).transpose(1, 0, 2)
     g_small = (

time: 492 us -> 448 us (0.911)
  Pallas kernels: 393 us -> 355 us
    pallas_call x3 -> x1, Pallas kernels: 187 us -> 152 us  [forward(): pl.pallas_call(functools.partial(forward_kernel, hi_count), out_shape=(sh...]
    another operation x0 -> x8, other arithmetic: none -> 5.3 us
  transfers between devices with their start and end apart: 2 -> 1, of which waited for: 1 -> 1; matrix products, arithmetic and copies ran while one was open for 3% -> 0% of each run, Pallas kernels for 27% -> 0%
where the time goes in v2:
time: 448 us; the launch traced here: 440 us
  Pallas kernels  355 us (79%)
  waiting for transfers between devices  44.6 us (10%)
  local copies, waits for them, and re-layouts  24.5 us (5%)
  other arithmetic  14.7 us (3%)
    pallas_call x1, Pallas kernels, forward(): pl.pallas_call(functools.partial(forward_kernel, hi_count), out_shape=(sh...  152 us
    pallas_call x1, Pallas kernels, scatter(): pl.pallas_call(functools.partial(scatter_kernel, hi_count), out_shape=(ja...  129 us
    ppermute x1, waiting for transfers between devices, local(): lax.ppermute(jnp.concatenate([d_k[rows:], d_v[rows:]], axis=1), 'rep', [(...  44.6 us
    pallas_call x1, Pallas kernels, backward(): pl.pallas_call(backward_kernel, grid=(CHUNKS,), out_shape=(jax.ShapeDtype...  33.1 us
    pallas_call x1, Pallas kernels, attend_back(): pl.pallas_call(attend_back_kernel, grid=(HEADS // 4,), out_shape=(jax.Sha...  27.1 us
    pallas_call x1, Pallas kernels, project_back(): pl.pallas_call(project_back_kernel, grid=(3 * per,), out_shape=(jax.Shape...  13.8 us
  transfers between devices with their start and end apart: 1, of which 1 were waited for; matrix products, arithmetic and copies ran while one was open for 0% of the time, Pallas kernels for 0%

profile of v2, /device:TPU:0, one launch (start us, length us, event | category | flops | bytes accessed | tf_op | source)
XLA Modules:
  0.0 440.4 jit_solution(16905209339286503550)
XLA Ops:
  0.7 1.5 fusion.q_doc
  2.1 0.7 convert.24
  4.8 0.7 convert.28
  7.6 0.7 tile.9.vec
  8.3 2.2 constant_dynamic-slice_fusion
  10.5 151.7 %forward.1 = (bf16[12,4,2,2,64,1024]{5,4,3,2,1,0:T(8,128)(2,1)}, bf16[4,512,256]{2,1,0:T(8,128)(2,1)}, bf16[4,1024,256]{2,1,0:T(8,128)(2,1)}, bf16[4,1024,256]{2...) custom-call(f32[64,3072]{1,0:T(8,128)} %w_qkv.1, ...), custom_call_target="tpu_custom_call" | custom-call | tf_op jit(solution)/shard_map/forward/pallas_call | solution.py:606
  162.2 33.1 %backward.1 = (bf16[4096,1024]{1,0:T(8,128)(2,1)}, bf16[1024,4096]{1,0:T(8,128)(2,1)}, f32[1,4096]{1,0:T(1,128)}, bf16[1024,1024]{1,0:T(8,128)(2,1)}, f32[512,10...) custom-call(bf16[512,1024]{1,0:T(8,128)(2,1)} %get-tuple-element.52.d_ffn, ...), custom_call_target="tpu_custom_call" | custom-call | tf_op jit(solution)/shard_map/backward/pallas_call | solution.py:1057
  195.3 27.1 %attend_back.1 = (bf16[512,1024]{1,0:T(8,128)(2,1)}, bf16[1024,1024]{1,0:T(8,128)(2,1)}, bf16[1024,1024]{1,0:T(8,128)(2,1)}) custom-call(bf16[4,512,256]{2,1,0:T(8,128)(2,1)} %get-tuple-element.48.q_in, bf16[4,1024,256]{2,1,0:T(8,128)(2,1)} %get-tuple-element.49.k_in, bf16[4,1024,256]{2,1,0:T(8,128)(2,1)} %get-tuple-element.50.v_in, ...), custom_call_target="tpu_custom_call" | custom-call | tf_op jit(solution)/shard_map/attend_back/pallas_call | solution.py:972
  222.4 1.9 fusion.2
  224.9 1.5 pad_maximum_fusion.1
  228.0 0.7 reduce.31
  228.9 44.6 %collective-permute-done = bf16[512,2048]{1,0:T(8,128)(2,1)} collective-permute-done((bf16[512,2048]{1,0:T(8,128)(2,1)}, bf16[512,2048]{1,0:T(8,128)(2,1)}, u32[]{:S(2)}, u32[]{:S(2)}) %collective-permute-start) | collective-permute-done | bytes 2097184 | tf_op jit(solution)/shard_map/ppermute | solution.py:1192
  273.5 2.4 add_convert_fusion
  275.9 1.9 pad_maximum_fusion.d_joined
  277.8 13.8 %project_back.1 = (bf16[1024,3072]{1,0:T(8,128)(2,1)}, f32[1,3072]{1,0:T(1,128)}, f32[512,1024]{1,0:T(8,128)}) custom-call(bf16[512,1024]{1,0:T(8,128)(2,1)} %tokens.3, bf16[512,3072]{1,0:T(8,128)(2,1)} %pad_maximum_fusion.d_joined, f32[512,1024]{1,0:T(8,128)} %get-tuple-element.67.d_resid, bf16[12,1024,1024]{2,1,0:T(8,128)(2,1)} %bitcast.24), custom_call_target="tpu_custom_call" | custom-call | tf_op jit(solution)/shard_map/project_back/pallas_call | solution.py:1118
  291.6 1.4 reduce.30
  293.8 129.1 %scatter.1 = (f32[12,64,1024]{2,1,0:T(8,128)}, f32[8,128]{1,0:T(8,128)}) custom-call(bf16[4,2,2,64,3072]{4,3,2,1,0:T(8,128)(2,1)} %bitcast.28, bf16[4,2,2,64,1024]{4,3,2,1,0:T(8,128)(2,1)} %bitcast.29, bf16[4,2,2,64,4096]{4,3,2,1,0:T(8,128)(2,1)} %bitcast.26, bf16[4,4,2,2,64,1024]{5,4,3,2,1,0:T(8,128)(2,1)} %bitcast.25, f32[4,2,2,8,128]{4,3,2,1,0:T(8,128)} %bitcast.32), custom_call_target="tpu_custom_call" | custom-call | tf_op jit(solution)/shard_map/scatter/pallas_call | solution.py:880
  422.9 2.7 fusion.1
  425.6 2.1 slice_bitcast_fusion
  427.7 1.7 slice_bitcast_fusion.1
  431.7 2.7 copy.35
  434.4 3.6 reshape.89
  438.0 0.9 copy.36
  439.0 1.0 copy.39
  (47 shorter events, 9.5 us)
Async XLA Ops:
  222.4 2.2 copy-start.1
  224.8 2.1 copy-start.5
  224.8 2.1 copy-start.6
  224.8 3.1 copy-start.4
  226.4 47.1 %collective-permute-start = (bf16[512,2048]{1,0:T(8,128)(2,1)}, bf16[512,2048]{1,0:T(8,128)(2,1)}, u32[]{:S(2)}, u32[]{:S(2)}) collective-permute-start(bf16[512,2048]{1,0:T(8,128)(2,1)} %pad_maximum_fusion.1), channel_id=1, source_target_pairs={{0,16},{16,0},{1,17},{17,1},{2,18},{18,2},{3,19},{19,3},{4,20},{20... | collective-permute-start | bytes 6291464 | tf_op jit(solution)/shard_map/ppermute | solution.py:1192
  273.5 2.5 copy-start.3
  422.9 6.5 %copy-start.7 = (f32[8,128]{1,0:T(8,128)S(1)}, f32[8,128]{1,0:T(8,128)}, u32[]{:S(2)}) copy-start(f32[8,128]{1,0:T(8,128)} %get-tuple-element.78) | copy-start | bytes 12292
  431.7 6.3 %copy-start = (f32[3,8,8,1024]{3,2,1,0:T(8,128)S(1)}, f32[3,8,8,1024]{3,2,1,0:T(8,128)}, u32[]{:S(2)}) copy-start(f32[3,8,8,1024]{3,2,1,0:T(8,128)} %slice_bitcast_fusion) | copy-start | bytes 2359300
  434.4 4.6 %copy-start.2 = (bf16[512,1024]{1,0:T(8,128)(2,1)S(1)}, bf16[512,1024]{1,0:T(8,128)(2,1)}, u32[]{:S(2)}) copy-start(bf16[512,1024]{1,0:T(8,128)(2,1)} %get-tuple-element.116) | copy-start | bytes 3145732
